TPU v7x, 1024 devices: a whole 4x8x16 slice. The times are simulated.
1024 devices in a mesh: blk: 128 (over y_lo, z, core), grp: 8 (over x, y_hi).
Axes of the slice: x: 4, y: 8 (y_hi: 2, y_lo: 4; y = y_hi * 4 + y_lo), z: 16, core: 2. Of those that a mesh axis runs over, the one named last changes fastest.
Arguments:
- embeddings: bfloat16 [196608, 1280], P(('blk', 'grp')), may hold values from -48 to 48
- proj_weight: bfloat16 [1280, 1024], replicated, may hold values from -0.15625 to 0.15625
- labels: int32 [196608], replicated, may hold values from 0 to 3071
- flags: int32 [196608], replicated, may hold values 0 or 1
Outputs:
- row_loss: float32 [196608], P(('blk', 'grp'))
- head_grad: float32 [1280, 1024], P('blk', 'grp')
All inputs are finite; a program needn't handle non-finite values.
Results may differ from a plain program's by a relative error of at most 0.0019.
Values may be sent and summed in bfloat16 or wider, within the bound.
A program may use at most 64 MiB of HBM per device.

v0:
```python
import jax
import jax.numpy as jnp
from jax import lax
from jax.sharding import PartitionSpec as P

SOFTMAX_TEMP = 0.1


def passed_along(block, axis, distance):
    devices = range(lax.axis_size(axis))
    route = [((i - distance) % len(devices), i) for i in devices]
    return lax.ppermute(block, axis, route)


def on_device(embeddings, proj_weight, labels, flags):
    rows = embeddings.shape[0]
    blocks = lax.axis_size("blk")
    group = lax.axis_size("grp")
    blk_id = lax.axis_index("blk")
    grp_id = lax.axis_index("grp")
    half = min(4, blocks // 2 - 1)
    span = 2 * half + 1
    width_c = span * rows
    z = jnp.dot(embeddings, proj_weight, preferred_element_type=jnp.float32)
    norm = jnp.sqrt(jnp.sum(z * z, axis=1, keepdims=True) + 1e-06)
    zn = z / norm
    unit_embeddings = zn.astype(jnp.bfloat16)
    own_start = blk_id * rows * group + grp_id * rows
    own_ids = own_start + jnp.arange(rows, dtype=jnp.int32)
    own_lab = lax.dynamic_slice_in_dim(labels, own_start, rows, 0)
    weight_all = jnp.where(flags == 1, 0.5, 1.0).astype(jnp.float32)
    own_w = lax.dynamic_slice_in_dim(weight_all, own_start, rows, 0)
    place = jnp.arange(width_c, dtype=jnp.int32)
    col_blk = (blk_id + place // rows - half) % blocks
    col_ids = col_blk * rows * group + grp_id * rows + place % rows
    col_lab = jnp.take(labels, col_ids)
    col_w = jnp.take(weight_all, col_ids)
    notself = own_ids[:, None] != col_ids[None, :]
    same = jnp.logical_and(own_lab[:, None] == col_lab[None, :], notself)
    samef = same.astype(jnp.float32)
    unit_pieces = []
    for offset in range(-half, half + 1):
        if offset == 0:
            unit_pieces.append(unit_embeddings)
        else:
            unit_pieces.append(passed_along(unit_embeddings, "blk", -offset))
    block_window = jnp.concatenate(unit_pieces, axis=0)
    similarity_scores = (
        jnp.dot(unit_embeddings, block_window.T, preferred_element_type=jnp.float32) / SOFTMAX_TEMP
    )
    expo = jnp.where(notself, jnp.exp(similarity_scores), 0.0)
    denom = jnp.sum(expo, axis=1)
    possum = jnp.sum(jnp.where(same, similarity_scores, 0.0), axis=1)
    count = jnp.sum(samef, axis=1)
    inv_count = 1.0 / jnp.maximum(count, 1.0)
    recip = 1.0 / denom
    row_loss = own_w * (jnp.log(denom) - possum * inv_count)
    stats = jnp.stack([recip, inv_count], axis=1)
    stat_pieces = []
    for offset in range(-half, half + 1):
        if offset == 0:
            stat_pieces.append(stats)
        else:
            stat_pieces.append(passed_along(stats, "blk", -offset))
    col_stats = jnp.concatenate(stat_pieces, axis=0)
    col_recip = col_stats[:, 0]
    col_inv = col_stats[:, 1]
    row_coefficient = own_w[:, None] * (expo * recip[:, None] - samef * inv_count[:, None])
    column_coefficient = col_w[None, :] * (expo * col_recip[None, :] - samef * col_inv[None, :])
    pair_logits = ((row_coefficient + column_coefficient) / SOFTMAX_TEMP).astype(jnp.bfloat16)
    grad_unit = jnp.dot(pair_logits, block_window, preferred_element_type=jnp.float32)
    grad_z = (grad_unit - zn * jnp.sum(zn * grad_unit, axis=1, keepdims=True)) / norm
    grad_zb = grad_z.astype(jnp.bfloat16)
    partial_grad = jnp.dot(embeddings.T, grad_zb, preferred_element_type=jnp.float32)
    reduced = lax.psum_scatter(partial_grad, "blk", scatter_dimension=0, tiled=True)
    head_grad = lax.psum_scatter(reduced, "grp", scatter_dimension=1, tiled=True)
    return (row_loss, head_grad)


def solution(mesh):
    return jax.shard_map(
        on_device,
        mesh=mesh,
        in_specs=(P(("blk", "grp"), None), P(), P(), P()),
        out_specs=(P(("blk", "grp")), P("blk", "grp")),
        check_vma=False,
    )
```

profile of v0, /device:TPU:2, one launch (start us, length us, event | category | flops | bytes accessed | tf_op | source)
XLA Modules:
  0.0 1377.2 jit_solution(5131144531213720548)
XLA Ops:
  7.2 1.7 copy-done
  8.9 1.8 multiply_reduce_fusion.1
  12.5 6.1 collective-permute-start
  18.6 3.4 collective-permute-start.1
  22.0 5.5 collective-permute-start.2
  27.5 4.4 collective-permute-start.3
  31.9 9.0 collective-permute-start.4
  40.9 1.2 compare_select_fusion.1
  42.2 57.7 %gather_fusion = s32[1728]{0:T(1024)S(1)} fusion(s32[196608]{0:T(1024)} %param.6, s32[2048]{0:T(1024)S(1)} %pad_clamp_fusion), kind=kCustom, calls=%fused_computation | custom fusion | bytes 20736 | tf_op jit(solution)/shard_map/jit(_take)/gather | solution.py:36
  100.8 5.7 collective-permute-start.5
  107.5 4.3 collective-permute-start.6
  112.9 6.0 collective-permute-start.7
  122.2 9.7 collective-permute-done.6
  131.9 12.9 collective-permute-done.7
  144.8 3.8 fusion
  149.3 4.5 collective-permute-start.8
  153.8 1.9 collective-permute-start.9
  155.7 2.2 collective-permute-start.10
  158.0 9.4 gather_fusion.1
  167.4 1.9 collective-permute-start.11
  169.3 7.5 collective-permute-start.12
  176.9 3.6 collective-permute-start.13
  180.5 2.7 collective-permute-start.14
  183.3 4.0 collective-permute-start.15
  187.4 2.3 collective-permute-done.15
  189.8 4.1 multiply_reduce_fusion
  194.0 3.4 convolution_bitcast_fusion
  197.5 1.3 dynamic-slice
  199.4 1075.9 %all-reduce.3.cloned.1.call-done = f32[1280,1024]{0,1:T(8,128)} async-done(((f32[1280,1024]{0,1:T(8,128)}), f32[1280,1024]{0,1:T(8,128)}) %all-reduce.3.cloned.1.call-update) | async-done | bytes 5242896
  1275.3 2.2 constant_dynamic-slice_fusion
  1277.6 91.3 %reduce-scatter.3.cloned.1.call-done = f32[10,128]{0,1:T(8,128)} async-done(((f32[10,1024]{0,1:T(8,128)}), f32[10,128]{0,1:T(8,128)}) %reduce-scatter.3.cloned.1.call-update) | async-done | bytes 5136 | tf_op jit(solution)/shard_map/reduce_scatter | solution.py:76
  1368.8 1.5 copy.8
  (49 shorter events, 9.0 us)
Async XLA Ops:
  7.2 1.7 copy-start
  7.2 1268.1 %all-reduce.3.cloned.1.call-start = ((), (), s32[]{:S(2)}) async-start(), calls=%async_computation.2 | async-start | bytes 10485760
  10.7 0.9 copy-start.1
  12.5 88.3 %collective-permute-start = (bf16[192,1024]{1,0:T(8,128)(2,1)}, bf16[192,1024]{1,0:T(8,128)(2,1)}, u32[]{:S(2)}, u32[]{:S(2)}) collective-permute-start(bf16[192,1024]{1,0:T(8,128)(2,1)} %fusion.38), channel_id=1, source_target_pairs={{992,0},{1000,8},{1008,16},{1016,24},{0,32},{8,40},{16,48},{24,56}... | collective-permute-start | bytes 1179656 | tf_op jit(solution)/shard_map/ppermute | solution.py:12
  18.6 88.9 %collective-permute-start.1 = (bf16[192,1024]{1,0:T(8,128)(2,1)}, bf16[192,1024]{1,0:T(8,128)(2,1)}, u32[]{:S(2)}, u32[]{:S(2)}) collective-permute-start(bf16[192,1024]{1,0:T(8,128)(2,1)} %fusion.38), channel_id=1, source_target_pairs={{1000,0},{1008,8},{1016,16},{0,24},{8,32},{16,40},{24,48},{32,56},... | collective-permute-start | bytes 1179656 | tf_op jit(solution)/shard_map/ppermute | solution.py:12
  22.0 90.9 %collective-permute-start.2 = (bf16[192,1024]{1,0:T(8,128)(2,1)}, bf16[192,1024]{1,0:T(8,128)(2,1)}, u32[]{:S(2)}, u32[]{:S(2)}) collective-permute-start(bf16[192,1024]{1,0:T(8,128)(2,1)} %fusion.38), channel_id=1, source_target_pairs={{1008,0},{1016,8},{0,16},{8,24},{16,32},{24,40},{32,48},{40,56},{4... | collective-permute-start | bytes 1179656 | tf_op jit(solution)/shard_map/ppermute | solution.py:12
  27.5 92.4 %collective-permute-start.3 = (bf16[192,1024]{1,0:T(8,128)(2,1)}, bf16[192,1024]{1,0:T(8,128)(2,1)}, u32[]{:S(2)}, u32[]{:S(2)}) collective-permute-start(bf16[192,1024]{1,0:T(8,128)(2,1)} %fusion.38), channel_id=1, source_target_pairs={{1016,0},{0,8},{8,16},{16,24},{24,32},{32,40},{40,48},{48,56},{56,... | collective-permute-start | bytes 1179656 | tf_op jit(solution)/shard_map/ppermute | solution.py:12
  31.9 89.2 %collective-permute-start.4 = (bf16[192,1024]{1,0:T(8,128)(2,1)}, bf16[192,1024]{1,0:T(8,128)(2,1)}, u32[]{:S(2)}, u32[]{:S(2)}) collective-permute-start(bf16[192,1024]{1,0:T(8,128)(2,1)} %fusion.38), channel_id=1, source_target_pairs={{8,0},{16,8},{24,16},{32,24},{40,32},{48,40},{56,48},{64,56},{72,6... | collective-permute-start | bytes 1179656 | tf_op jit(solution)/shard_map/ppermute | solution.py:12
  100.0 21.0 %copy-start.2 = (f32[192,1024]{1,0:T(8,128)S(1)}, f32[192,1024]{1,0:T(8,128)}, u32[]{:S(2)}) copy-start(f32[192,1024]{1,0:T(8,128)} %copy-done.1) | copy-start | bytes 2359300
  100.8 21.4 %collective-permute-start.5 = (bf16[192,1024]{1,0:T(8,128)(2,1)}, bf16[192,1024]{1,0:T(8,128)(2,1)S(1)}, u32[]{:S(2)}, u32[]{:S(2)}) collective-permute-start(bf16[192,1024]{1,0:T(8,128)(2,1)} %fusion.38), channel_id=1, source_target_pairs={{16,0},{24,8},{32,16},{40,24},{48,32},{56,40},{64,48},{72,56},{80,... | collective-permute-start | bytes 1179656 | tf_op jit(solution)/shard_map/ppermute | solution.py:12
  107.5 24.4 %collective-permute-start.6 = (bf16[192,1024]{1,0:T(8,128)(2,1)}, bf16[192,1024]{1,0:T(8,128)(2,1)S(1)}, u32[]{:S(2)}, u32[]{:S(2)}) collective-permute-start(bf16[192,1024]{1,0:T(8,128)(2,1)} %fusion.38), channel_id=1, source_target_pairs={{24,0},{32,8},{40,16},{48,24},{56,32},{64,40},{72,48},{80,56},{88,... | collective-permute-start | bytes 1179656 | tf_op jit(solution)/shard_map/ppermute | solution.py:12
  112.9 31.9 %collective-permute-start.7 = (bf16[192,1024]{1,0:T(8,128)(2,1)}, bf16[192,1024]{1,0:T(8,128)(2,1)S(1)}, u32[]{:S(2)}, u32[]{:S(2)}) collective-permute-start(bf16[192,1024]{1,0:T(8,128)(2,1)} %fusion.38), channel_id=1, source_target_pairs={{32,0},{40,8},{48,16},{56,24},{64,32},{72,40},{80,48},{88,56},{96,... | collective-permute-start | bytes 1179656 | tf_op jit(solution)/shard_map/ppermute | solution.py:12
  144.8 3.9 copy-start.4
  149.3 27.5 %collective-permute-start.8 = (f32[192,2]{0,1:T(2,128)S(1)}, f32[192,2]{0,1:T(2,128)S(1)}, u32[]{:S(2)}, u32[]{:S(2)}) collective-permute-start(f32[192,2]{0,1:T(2,128)S(1)} %pad_maximum_fusion), channel_id=1, source_target_pairs={{992,0},{1000,8},{1008,16},{1016,24},{0,32},{8,40},{16,48},{24,56}... | collective-permute-start | bytes 4616 | tf_op jit(solution)/shard_map/ppermute | solution.py:12
  153.8 26.7 %collective-permute-start.9 = (f32[192,2]{0,1:T(2,128)S(1)}, f32[192,2]{0,1:T(2,128)S(1)}, u32[]{:S(2)}, u32[]{:S(2)}) collective-permute-start(f32[192,2]{0,1:T(2,128)S(1)} %pad_maximum_fusion), channel_id=1, source_target_pairs={{1000,0},{1008,8},{1016,16},{0,24},{8,32},{16,40},{24,48},{32,56},... | collective-permute-start | bytes 4616 | tf_op jit(solution)/shard_map/ppermute | solution.py:12
  155.7 27.5 %collective-permute-start.10 = (f32[192,2]{0,1:T(2,128)S(1)}, f32[192,2]{0,1:T(2,128)S(1)}, u32[]{:S(2)}, u32[]{:S(2)}) collective-permute-start(f32[192,2]{0,1:T(2,128)S(1)} %pad_maximum_fusion), channel_id=1, source_target_pairs={{1008,0},{1016,8},{0,16},{8,24},{16,32},{24,40},{32,48},{40,56},{4... | collective-permute-start | bytes 4616 | tf_op jit(solution)/shard_map/ppermute | solution.py:12
  167.4 20.0 %collective-permute-start.11 = (f32[192,2]{0,1:T(2,128)S(1)}, f32[192,2]{0,1:T(2,128)S(1)}, u32[]{:S(2)}, u32[]{:S(2)}) collective-permute-start(f32[192,2]{0,1:T(2,128)S(1)} %pad_maximum_fusion), channel_id=1, source_target_pairs={{1016,0},{0,8},{8,16},{16,24},{24,32},{32,40},{40,48},{48,56},{56,... | collective-permute-start | bytes 4616 | tf_op jit(solution)/shard_map/ppermute | solution.py:12
  169.3 18.1 %collective-permute-start.12 = (f32[192,2]{0,1:T(2,128)S(1)}, f32[192,2]{0,1:T(2,128)S(1)}, u32[]{:S(2)}, u32[]{:S(2)}) collective-permute-start(f32[192,2]{0,1:T(2,128)S(1)} %pad_maximum_fusion), channel_id=1, source_target_pairs={{8,0},{16,8},{24,16},{32,24},{40,32},{48,40},{56,48},{64,56},{72,6... | collective-permute-start | bytes 4616 | tf_op jit(solution)/shard_map/ppermute | solution.py:12
  176.9 10.5 collective-permute-start.13
  180.5 6.9 collective-permute-start.14
  183.3 6.4 collective-permute-start.15
  189.8 4.2 copy-start.3
  189.8 4.2 copy-start.5
  197.4 1171.4 %reduce-scatter.3.cloned.1.call-start = ((), (), s32[]{:S(2)}) async-start(), calls=%async_computation.1 | async-start | bytes 589824 | tf_op jit(solution)/shard_map/reduce_scatter | solution.py:76
Sparse Core Ops, SparseCore 0:
  197.5 1077.7 all-reduce.2
  1281.9 86.9 reduce-scatter.2
where the time goes:
time: 1380 us
  waiting for transfers between devices  1190 us (86%)
  local copies, waits for them, and re-layouts  80.9 us (6%)
  starting transfers between devices  72.9 us (5%)
  between operations  15.1 us (1%)
    unnamed x3, waiting for transfers between devices  1080 us
    reduce_scatter x1, waiting for transfers between devices, on_device(): lax.psum_scatter(reduced, 'grp', scatter_dimension=1, tiled=True)  91.3 us
    ppermute x16, starting transfers between devices, passed_along(): return lax.ppermute(block, axis, route)  72.9 us
    gather x1, local copies, waits for them, and re-layouts, on_device(): col_lab = jnp.take(labels, col_ids)  57.7 us
  transfers between devices with their start and end apart: 18, of which 5 were waited for; matrix products, arithmetic and copies ran while one was open for 6% of the time, Pallas kernels for 0%

commit v1 on v0

v1 whole, which is shorter than its diff:
```python
import functools

import jax
import jax.numpy as jnp
from jax import lax
from jax.experimental import pallas as pl
from jax.experimental.pallas import tpu as pltpu
from jax.sharding import PartitionSpec as P

MESH = pl.DeviceIdType.MESH
F32 = jnp.float32
BF16 = jnp.bfloat16

NX, NYH, NYL, NZ = 4, 2, 4, 16
NY = NYH * NYL
ROWS, E, WIDTH = 192, 1280, 1024
SLOTS = 9
PIECES = 4
PIECE = ROWS // PIECES
HALFROWS = ROWS // 2
SLICE = 128
YROWS = E // NYL // 2
ZROWS = 10
ZPAD = 16
SCALE = 10.0
YTYPE = F32


def kernel(
    emb_hbm, w_hbm, lab_hbm, flag_hbm, loss_ref, head_ref,
    w_v, lab_v, flag_v, lw, embg, zn, win, ex, pr, st, gu, gzs, gzg, part, yb, ysum, zs, zb,
    load_sem, halo_send, halo_recv, x_send, x_recv, st_send, st_recv,
    g_send, g_recv, y_send, y_recv, z_send, z_recv,
):
    blk = lax.axis_index("blk")
    grp = lax.axis_index("grp")
    blocks = 2 * NYL * NZ
    core = lax.rem(blk, 2)
    chip = blk // 2
    z_me = lax.rem(chip, NZ)
    yl_me = chip // NZ
    x_me = grp // NYH
    yh_me = lax.rem(grp, NYH)
    y_me = yh_me * NYL + yl_me
    own_x = x_me * 2 + core

    def wrap(value, size):
        return lax.rem(value + size, size)

    def chip_peer(step, which):
        return wrap(chip + step, blocks // 2) * 2 + which, grp

    def x_peer(step, which):
        return chip * 2 + which, wrap(x_me + step, NX) * NYH + yh_me

    sibling = (chip * 2 + 1 - core, grp)
    z_core = z_me // (NZ // 2)

    def remote(src, dst, send, recv, device):
        return pltpu.make_async_remote_copy(
            src_ref=src, dst_ref=dst, send_sem=send, recv_sem=recv, device_id=device, device_id_type=MESH
        )

    own_rows = pl.ds(pl.multiple_of(own_x * ROWS, 16), ROWS)
    loads = [pltpu.make_async_copy(emb_hbm, embg.at[own_rows, :], load_sem.at[0])]
    for n in range(4):
        columns = pl.ds(n * 256, 256)
        loads.append(pltpu.make_async_copy(w_hbm.at[:, columns], w_v.at[:, columns], load_sem.at[1 + n]))
    loads.append(pltpu.make_async_copy(lab_hbm, lab_v, load_sem.at[5]))
    loads.append(pltpu.make_async_copy(flag_hbm, flag_v, load_sem.at[6]))
    for load in loads:
        load.start()

    barrier = pltpu.get_barrier_semaphore()

    def greet(device):
        pl.semaphore_signal(barrier, inc=1, device_id=device, device_id_type=MESH)

    for step in (1, -1, 2, -2, 3, -3, 4, -4):
        greet((wrap(blk + step, blocks), grp))
    for step in (1, 2, 3):
        for which in (0, 1):
            greet(x_peer(step, which))

    def greet_y(y_src, carry):
        @pl.when(jnp.logical_or(y_src != y_me, core != yh_me))
        def _():
            greet(((lax.rem(y_src, NYL) * NZ + z_me) * 2 + yh_me, x_me * NYH + y_src // NYL))
        return carry

    lax.fori_loop(0, NY, greet_y, 0)

    def greet_z(z_src, carry):
        @pl.when(jnp.logical_or(z_src != z_me, core != z_core))
        def _():
            greet(((yl_me * NZ + z_src) * 2 + z_core, grp))
        return carry

    lax.fori_loop(0, NZ, greet_z, 0)

    loads[0].wait()
    emb = embg[own_rows, :]
    ssq = jnp.zeros((ROWS, 1), F32)
    for n in range(4):
        columns = pl.ds(n * 256, 256)
        loads[1 + n].wait()
        zc = jnp.dot(emb, w_v[:, columns], preferred_element_type=F32)
        zn[:, columns] = zc
        ssq = ssq + jnp.sum(zc * zc, axis=1, keepdims=True)
    rnorm = 1.0 / jnp.sqrt(ssq + 1e-6)
    for n in range(4):
        columns = pl.ds(n * 256, 256)
        zc = zn[:, columns] * rnorm
        zn[:, columns] = zc
        win[4, :, columns] = zc.astype(BF16)

    greeted = (
        8 + 6 + NY + NZ
        - jnp.where(core == yh_me, 1, 0).astype(jnp.int32)
        - jnp.where(core == z_core, 1, 0).astype(jnp.int32)
    )
    pl.semaphore_wait(barrier, greeted)

    ahead, behind = chip_peer(1, core), chip_peer(-1, core)
    sends = []

    def halo(src_slot, dst_slot, p, send, device):
        rows = pl.ds(p * PIECE, PIECE)
        copy = remote(
            win.at[src_slot, rows, :], win.at[dst_slot, rows, :],
            halo_send.at[send, p], halo_recv.at[dst_slot, p], device,
        )
        copy.start()
        sends.append(copy)

    def halo_wait(slot, p):
        rows = pl.ds(p * PIECE, PIECE)
        remote(
            win.at[slot, rows, :], win.at[slot, rows, :],
            halo_send.at[0, p], halo_recv.at[slot, p], sibling,
        ).wait_recv()

    for p in range(PIECES):
        halo(4, 2, p, 0, ahead)
        halo(4, 6, p, 1, behind)
        halo(4, 3 + 2 * core, p, 2, sibling)

    right, left = x_peer(1, core), x_peer(-1, core)

    def slot_rows(x_step, which, half=None):
        start = (wrap(x_me + x_step, NX) * 2 + which) * ROWS
        if half is None:
            return pl.ds(pl.multiple_of(start, 16), ROWS)
        return pl.ds(pl.multiple_of(start + half * HALFROWS, 16), HALFROWS)

    def x_copy(rows, send, recv, half, device):
        copy = remote(embg.at[rows, :], embg.at[rows, :], x_send.at[send], x_recv.at[recv, half], device)
        copy.start()
        sends.append(copy)

    def x_wait(rows, recv, half):
        remote(embg.at[rows, :], embg.at[rows, :], x_send.at[0], x_recv.at[recv, half], sibling).wait_recv()

    x_copy(own_rows, 0, 0, 0, sibling)
    x_copy(own_rows, 1, 1, 0, right)
    x_copy(own_rows, 2, 2, 0, left)

    loads[5].wait()
    loads[6].wait()
    odd = lax.rem(grp, 2) == 1

    def label_row(ref, block):
        row = block * 12 + (3 * grp) // 2
        return ref[pl.ds(row, 1), :].astype(F32), ref[pl.ds(row + 1, 1), :].astype(F32)

    lw[...] = jnp.zeros_like(lw)
    for slot in range(SLOTS):
        low, high = label_row(lab_v, wrap(blk + slot - 4, blocks))
        lw[slot : slot + 1, 0:128] = low
        lw[slot : slot + 1, 128:256] = high
    low, high = label_row(flag_v, blk)
    lw[SLOTS : SLOTS + 1, 0:128] = low
    lw[SLOTS : SLOTS + 1, 128:256] = high
    plain = lw[...]
    lw[...] = jnp.where(odd, pltpu.roll(plain, 192, 1), plain)
    turned = jnp.transpose(jnp.concatenate([lw[...], jnp.zeros((112, 256), F32)], axis=0))
    own_lab = turned[:ROWS, 4:5]
    own_w = jnp.where(turned[:ROWS, SLOTS : SLOTS + 1] == 1.0, 0.5, 1.0)
    diagonal = lax.broadcasted_iota(jnp.int32, (ROWS, ROWS), 0) == lax.broadcasted_iota(
        jnp.int32, (ROWS, ROWS), 1
    )

    def same_label(slot, own):
        same = own_lab == lw[pl.ds(slot, 1), :ROWS]
        return jnp.logical_and(same, jnp.logical_not(diagonal)) if own else same

    own_unit = win[4]

    def scores(slot, sums, own=False):
        denom, possum, count = sums
        s = SCALE * lax.dot_general(
            own_unit, win[slot], (((1,), (1,)), ((), ())), preferred_element_type=F32
        )
        e = jnp.exp(s)
        if own:
            e = jnp.where(diagonal, 0.0, e)
        same = same_label(slot, own)
        ex[slot] = e
        denom = denom + jnp.sum(e, axis=1, keepdims=True)
        possum = possum + jnp.sum(jnp.where(same, s, 0.0), axis=1, keepdims=True)
        count = count + jnp.sum(jnp.where(same, 1.0, 0.0), axis=1, keepdims=True)
        return denom, possum, count

    nought = jnp.zeros((ROWS, 1), F32)
    sums = scores(4, (nought, nought, nought), own=True)

    for p in range(PIECES):
        halo_wait(2, p)
        halo(2, 0, p, 3, ahead)
        halo(2, 1 + 2 * core, p, 4, sibling)
        halo_wait(6, p)
        halo(6, 8, p, 5, behind)
        halo(6, 5 + 2 * core, p, 6, sibling)
    sums = scores(2, sums)
    sums = scores(6, sums)
    for slot in (5 - 2 * core, 3 - 2 * core, 7 - 2 * core):
        for p in range(PIECES):
            halo_wait(slot, p)
        sums = scores(slot, sums)

    x_wait(slot_rows(-1, core), 1, 0)
    x_copy(slot_rows(-1, core, 0), 3, 3, 0, right)
    x_copy(slot_rows(-1, core), 5, 4, 0, sibling)
    x_wait(slot_rows(1, core), 2, 0)
    x_copy(slot_rows(1, core, 1), 4, 3, 1, left)
    x_copy(slot_rows(1, core), 6, 5, 0, sibling)

    for p in range(PIECES):
        halo_wait(8 - 8 * core, p)
        halo(8 - 8 * core, 7 - 6 * core, p, 7, sibling)
    sums = scores(8 - 8 * core, sums)
    for slot in (8 * core, 1 + 6 * core):
        for p in range(PIECES):
            halo_wait(slot, p)
        sums = scores(slot, sums)

    denom, possum, count = sums
    inv_count = 1.0 / jnp.maximum(count, 1.0)
    own_loss = own_w * (jnp.log(denom) - possum * inv_count)
    own_a = (SCALE * own_w) / denom
    own_c = (SCALE * own_w) * inv_count
    lane = lax.broadcasted_iota(jnp.int32, (ROWS, 128), 1)
    columns = jnp.where(lane == 0, own_a, jnp.where(lane == 1, own_c, own_loss))
    flat = jnp.transpose(jnp.concatenate([columns, jnp.zeros((64, 128), F32)], axis=0))
    st[4] = flat[:8]
    loss_ref[...] = flat[2:3]
    steps = (4, -4, 3, -3, 2, -2, 1, -1)
    for i, step in enumerate(steps):
        copy = remote(
            st.at[4], st.at[4 - step], st_send.at[i], st_recv.at[4 - step], (wrap(blk + step, blocks), grp)
        )
        copy.start()
        sends.append(copy)

    for half in (0, 1):
        x_wait(slot_rows(2, core, half), 3, half)
        x_copy(slot_rows(2, core, half), 7 + half, 6, half, sibling)

    def pairs(slot, own=False):
        row = st[slot]
        same = same_label(slot, own)
        value = ex[slot] * (own_a + row[0:1, :ROWS]) - jnp.where(same, own_c + row[1:2, :ROWS], 0.0)
        pr[slot] = value.astype(BF16)

    pairs(4, own=True)
    for step in (1, -1, 2, -2, 3, -3, 4, -4):
        slot = 4 + step
        remote(st.at[slot], st.at[slot], st_send.at[0], st_recv.at[slot], sibling).wait_recv()
        pairs(slot)

    along = jnp.zeros((ROWS, 1), F32)
    for n in range(4):
        columns = pl.ds(n * 256, 256)
        total = jnp.dot(pr[0], win[0, :, columns], preferred_element_type=F32)
        for slot in range(1, SLOTS):
            total = total + jnp.dot(pr[slot], win[slot, :, columns], preferred_element_type=F32)
        gu[:, columns] = total
        along = along + jnp.sum(zn[:, columns] * total, axis=1, keepdims=True)
    for j in range(2 * NX):
        columns = pl.ds(j * SLICE, SLICE)
        gzs[j] = ((gu[:, columns] - zn[:, columns] * along) * rnorm).astype(BF16)
    g_sends = []
    for step in (2, 1, 3, 0):
        for which in (0, 1):
            if step == 0 and which == 0:
                target, device = x_me * 2 + 1 - core, sibling
            elif step == 0:
                continue
            else:
                target, device = wrap(x_me + step, NX) * 2 + which, x_peer(step, which)
            copy = remote(
                gzs.at[target], gzg.at[own_rows, :], g_send.at[2 * step + which], g_recv.at[own_x], device
            )
            copy.start()
            sends.append(copy)
    gzg[own_rows, :] = gzs[own_x]

    x_wait(slot_rows(0, 1 - core), 0, 0)
    x_wait(slot_rows(-1, 1 - core), 4, 0)
    x_wait(slot_rows(1, 1 - core), 5, 0)
    for half in (0, 1):
        x_wait(slot_rows(2, 1 - core, half), 6, half)
    for step, which in ((0, 1 - core), (1, 0), (1, 1), (3, 0), (3, 1), (2, 0), (2, 1)):
        source = wrap(x_me + step, NX) * 2 + which
        rows = slot_rows(step, which)
        remote(gzs.at[0], gzg.at[rows, :], g_send.at[0], g_recv.at[source], sibling).wait_recv()

    for n in range(E // 256):
        columns = pl.ds(n * 256, 256)
        piece = lax.dot_general(
            gzg[...], embg[:, columns], (((0,), (0,)), ((), ())), preferred_element_type=F32
        )
        part[pl.ds(n * 256, 256), :] = jnp.transpose(piece).astype(YTYPE)

    def y_rows(yl, which):
        return pl.ds(yl * (2 * YROWS) + which * YROWS, YROWS)

    def y_self(yl, which):
        return jnp.logical_and(core == yh_me, jnp.logical_and(yl_me == yl, core == which))

    def y_copy(yl, which):
        return remote(
            part.at[y_rows(yl, which), :], yb.at[y_me], y_send.at[yl, which], y_recv.at[y_me],
            ((yl * NZ + z_me) * 2 + which, x_me * NYH + core),
        )

    for yl in range(NYL):
        for which in (0, 1):
            @pl.when(jnp.logical_not(y_self(yl, which)))
            def _(yl=yl, which=which):
                y_copy(yl, which).start()

            @pl.when(y_self(yl, which))
            def _(yl=yl, which=which):
                yb[y_me] = part[y_rows(yl, which), :]

    for src in range(NY):
        @pl.when(jnp.logical_or(y_me != src, core != yh_me))
        def _(src=src):
            remote(yb.at[src], yb.at[src], y_send.at[0, 0], y_recv.at[src], sibling).wait_recv()

    total = yb[0].astype(F32)
    for src in range(1, NY):
        total = total + yb[src].astype(F32)
    ysum[0:YROWS, :] = total
    ysum[YROWS:, :] = jnp.zeros((ZPAD, SLICE), F32)

    for i in range(NZ):
        zs[i] = ysum[i * ZROWS : i * ZROWS + ZPAD, :]

    def z_copy(i, which):
        return remote(
            zs.at[i * 2 + which], zb.at[z_me], z_send.at[i, which], z_recv.at[z_me],
            ((yl_me * NZ + core * (NZ // 2) + i) * 2 + which, grp),
        )

    def z_self(i, which):
        return jnp.logical_and(z_me == core * (NZ // 2) + i, core == which)

    for i in range(NZ // 2):
        for which in (0, 1):
            @pl.when(jnp.logical_not(z_self(i, which)))
            def _(i=i, which=which):
                z_copy(i, which).start()

            @pl.when(z_self(i, which))
            def _(i=i, which=which):
                zb[z_me] = zs[i * 2 + which]

    for src in range(NZ):
        @pl.when(jnp.logical_or(z_me != src, core != z_core))
        def _(src=src):
            remote(zb.at[src], zb.at[src], z_send.at[0, 0], z_recv.at[src], sibling).wait_recv()

    total = zb[0]
    for src in range(1, NZ):
        total = total + zb[src]
    head_ref[...] = total[:ZROWS, :]

    for copy in sends:
        copy.wait_send()
    for yl in range(NYL):
        for which in (0, 1):
            @pl.when(jnp.logical_not(y_self(yl, which)))
            def _(yl=yl, which=which):
                y_copy(yl, which).wait_send()
    for i in range(NZ // 2):
        for which in (0, 1):
            @pl.when(jnp.logical_not(z_self(i, which)))
            def _(i=i, which=which):
                z_copy(i, which).wait_send()


def on_device(embeddings, proj_weight, labels, flags):
    dma = pltpu.SemaphoreType.DMA
    loss, head = pl.pallas_call(
        kernel,
        out_shape=(
            jax.ShapeDtypeStruct((1, 256), F32),
            jax.ShapeDtypeStruct((ZROWS, SLICE), F32),
        ),
        in_specs=[pl.BlockSpec(memory_space=pl.ANY)] * 4,
        out_specs=(
            pl.BlockSpec(memory_space=pltpu.VMEM),
            pl.BlockSpec(memory_space=pltpu.VMEM),
        ),
        scratch_shapes=[
            pltpu.VMEM((E, WIDTH), BF16),
            pltpu.VMEM((1536, 128), jnp.int32),
            pltpu.VMEM((1536, 128), jnp.int32),
            pltpu.VMEM((16, 256), F32),
            pltpu.VMEM((2 * NX * ROWS, E), BF16),
            pltpu.VMEM((ROWS, WIDTH), F32),
            pltpu.VMEM((SLOTS, ROWS, WIDTH), BF16),
            pltpu.VMEM((SLOTS, ROWS, ROWS), F32),
            pltpu.VMEM((SLOTS, ROWS, ROWS), BF16),
            pltpu.VMEM((SLOTS, 8, 256), F32),
            pltpu.VMEM((ROWS, WIDTH), F32),
            pltpu.VMEM((2 * NX, ROWS, SLICE), BF16),
            pltpu.VMEM((2 * NX * ROWS, SLICE), BF16),
            pltpu.VMEM((E, SLICE), YTYPE),
            pltpu.VMEM((NY, YROWS, SLICE), YTYPE),
            pltpu.VMEM((YROWS + ZPAD, SLICE), F32),
            pltpu.VMEM((NZ, ZPAD, SLICE), F32),
            pltpu.VMEM((NZ, ZPAD, SLICE), F32),
            dma((7,)),
            dma((8, PIECES)),
            dma((SLOTS, PIECES)),
            dma((9,)),
            dma((7, 2)),
            dma((8,)),
            dma((SLOTS,)),
            dma((8,)),
            dma((2 * NX,)),
            dma((NYL, 2)),
            dma((NY,)),
            dma((NZ // 2, 2)),
            dma((NZ,)),
        ],
        compiler_params=pltpu.CompilerParams(
            collective_id=0, has_side_effects=True, vmem_limit_bytes=60 * 2**20
        ),
        name="contrastive_loss_and_head_gradient",
    )(embeddings, proj_weight, labels.reshape(1536, 128), flags.reshape(1536, 128))
    return loss[0, :ROWS], head


def solution(mesh):
    return jax.shard_map(
        on_device,
        mesh=mesh,
        in_specs=(P(("blk", "grp"), None), P(), P(), P()),
        out_specs=(P(("blk", "grp")), P("blk", "grp")),
        check_vma=False,
    )
```

time: 1380 us -> 84.8 us (0.06)
  the two profiles are of different devices: /device:TPU:2 before, /device:TPU:81 now
where the time goes in v1:
time: 84.8 us; the launch traced here: 84.6 us
  Pallas kernels  81.4 us (96%)
  local copies, waits for them, and re-layouts  2.51 us (3%)
    pallas_call x1, Pallas kernels, on_device(): pl.pallas_call(kernel, out_shape=(jax.ShapeDtypeStruct((1, 256), F32), ja...  81.4 us
    unnamed x2, local copies, waits for them, and re-layouts  2.51 us

profile of v1, /device:TPU:81, one launch (start us, length us, event | category | flops | bytes accessed | tf_op | source)
XLA Modules:
  0.0 84.6 jit_solution(14655931544929954594)
XLA Ops:
  0.6 81.4 %contrastive_loss_and_head_gradient.1 = (f32[1,256]{1,0:T(1,128)}, f32[10,128]{1,0:T(8,128)}) custom-call(bf16[192,1280]{1,0:T(8,128)(2,1)} %emb_hbm.1, bf16[1280,1024]{1,0:T(8,128)(2,1)} %w_hbm.1, s32[1536,128]{1,0:T(8,128)} %bitcast.4, s32[1536,128]{1,0:T(8,128)} %bitcast.5), custom_call_target="tpu_custom_call" | custom-call | tf_op jit(solution)/shard_map/contrastive_loss_and_head_gradient/pallas_call | solution.py:406
  82.0 1.2 %copy.8 = f32[192]{0:T(256)} copy(f32[192]{0:T(256)} %bitcast.6) | data formatting | bytes 1536
  83.3 1.3 %copy.9 = f32[10,128]{1,0:T(8,128)} copy(f32[10,128]{1,0:T(8,128)} %get-tuple-element.9) | data formatting | bytes 10240

commit v2 on v1

--- a/solution.py
+++ b/solution.py
@@ -20,16 +20,16 @@
 HALFROWS = ROWS // 2
 SLICE = 128
 YROWS = E // NYL // 2
+YPART = YROWS // 2
 ZROWS = 10
-ZPAD = 16
 SCALE = 10.0
-YTYPE = F32
+YTYPE = BF16
 
 
 def kernel(
     emb_hbm, w_hbm, lab_hbm, flag_hbm, loss_ref, head_ref,
-    w_v, lab_v, flag_v, lw, embg, zn, win, ex, pr, st, gu, gzs, gzg, part, yb, ysum, zs, zb,
-    load_sem, halo_send, halo_recv, x_send, x_recv, st_send, st_recv,
+    w_v, lab_v, flag_v, lw, embg, zn, win, ex, sc, pr, st, tp, tpr, gu, gzs, gzg, part, yb, ysum, zs, zb,
+    load_sem, halo_send, halo_recv, x_send, x_recv, st_send, st_recv, tp_send, tp_recv,
     g_send, g_recv, y_send, y_recv, z_send, z_recv,
 ):
     blk = lax.axis_index("blk")
@@ -99,28 +99,11 @@
     lax.fori_loop(0, NZ, greet_z, 0)
 
     loads[0].wait()
-    emb = embg[own_rows, :]
-    ssq = jnp.zeros((ROWS, 1), F32)
-    for n in range(4):
-        columns = pl.ds(n * 256, 256)
-        loads[1 + n].wait()
-        zc = jnp.dot(emb, w_v[:, columns], preferred_element_type=F32)
-        zn[:, columns] = zc
-        ssq = ssq + jnp.sum(zc * zc, axis=1, keepdims=True)
-    rnorm = 1.0 / jnp.sqrt(ssq + 1e-6)
-    for n in range(4):
-        columns = pl.ds(n * 256, 256)
-        zc = zn[:, columns] * rnorm
-        zn[:, columns] = zc
-        win[4, :, columns] = zc.astype(BF16)
-
     greeted = (
         8 + 6 + NY + NZ
         - jnp.where(core == yh_me, 1, 0).astype(jnp.int32)
         - jnp.where(core == z_core, 1, 0).astype(jnp.int32)
     )
-    pl.semaphore_wait(barrier, greeted)
-
     ahead, behind = chip_peer(1, core), chip_peer(-1, core)
     sends = []
 
@@ -140,10 +123,31 @@
             halo_send.at[0, p], halo_recv.at[slot, p], sibling,
         ).wait_recv()
 
-    for p in range(PIECES):
-        halo(4, 2, p, 0, ahead)
-        halo(4, 6, p, 1, behind)
-        halo(4, 3 + 2 * core, p, 2, sibling)
+    rnorms = []
+    for half in (0, 1):
+        rows = slice(half * HALFROWS, (half + 1) * HALFROWS)
+        emb = embg[pl.ds(pl.multiple_of(own_x * ROWS + half * HALFROWS, 16), HALFROWS), :]
+        ssq = jnp.zeros((HALFROWS, 1), F32)
+        for n in range(4):
+            columns = pl.ds(n * 256, 256)
+            if half == 0:
+                loads[1 + n].wait()
+            zc = jnp.dot(emb, w_v[:, columns], preferred_element_type=F32)
+            zn[rows, columns] = zc
+            ssq = ssq + jnp.sum(zc * zc, axis=1, keepdims=True)
+        rnorms.append(1.0 / jnp.sqrt(ssq + 1e-6))
+        for n in range(4):
+            columns = pl.ds(n * 256, 256)
+            zc = zn[rows, columns] * rnorms[half]
+            zn[rows, columns] = zc
+            win[4, rows, columns] = zc.astype(BF16)
+        if half == 0:
+            pl.semaphore_wait(barrier, greeted)
+        for p in range(half * (PIECES // 2), (half + 1) * (PIECES // 2)):
+            halo(4, 2, p, 0, ahead)
+            halo(4, 6, p, 1, behind)
+            halo(4, 3 + 2 * core, p, 2, sibling)
+    rnorm = jnp.concatenate(rnorms, axis=0)
 
     right, left = x_peer(1, core), x_peer(-1, core)
 
@@ -162,8 +166,10 @@
         remote(embg.at[rows, :], embg.at[rows, :], x_send.at[0], x_recv.at[recv, half], sibling).wait_recv()
 
     x_copy(own_rows, 0, 0, 0, sibling)
-    x_copy(own_rows, 1, 1, 0, right)
-    x_copy(own_rows, 2, 2, 0, left)
+    for i, half in enumerate((0, 1)):
+        x_copy(slot_rows(0, core, half), 1 + i, 1, half, right)
+    for i, half in enumerate((1, 0)):
+        x_copy(slot_rows(0, core, half), 3 + i, 2, half, left)
 
     loads[5].wait()
     loads[6].wait()
@@ -196,23 +202,41 @@
 
     own_unit = win[4]
 
+    def tile(slot, own=False):
+        s = SCALE * lax.dot_general(
+            own_unit, win[slot], (((1,), (1,)), ((), ())), preferred_element_type=F32
+        )
+        e = jnp.exp(s)
+        return s, jnp.where(diagonal, 0.0, e) if own else e
+
     def scores(slot, sums, own=False):
         denom, possum, count = sums
-        s = SCALE * lax.dot_general(
-            own_unit, win[slot], (((1,), (1,)), ((), ())), preferred_element_type=F32
-        )
-        e = jnp.exp(s)
-        if own:
-            e = jnp.where(diagonal, 0.0, e)
+        s, e = tile(slot, own)
         same = same_label(slot, own)
         ex[slot] = e
+        sc[slot] = s
         denom = denom + jnp.sum(e, axis=1, keepdims=True)
         possum = possum + jnp.sum(jnp.where(same, s, 0.0), axis=1, keepdims=True)
         count = count + jnp.sum(jnp.where(same, 1.0, 0.0), axis=1, keepdims=True)
         return denom, possum, count
 
+    def cross(rows_slots, slot):
+        found = None
+        for rows_slot in rows_slots:
+            s = SCALE * lax.dot_general(
+                win[rows_slot], win[slot], (((1,), (1,)), ((), ())), preferred_element_type=F32
+            )
+            same = turned[:ROWS, rows_slot : rows_slot + 1] == lw[slot : slot + 1, :ROWS]
+            sums = [
+                jnp.sum(value, axis=0, keepdims=True)
+                for value in (jnp.exp(s), jnp.where(same, s, 0.0), jnp.where(same, 1.0, 0.0))
+            ]
+            found = sums if found is None else [a + b for a, b in zip(found, sums)]
+        return found
+
     nought = jnp.zeros((ROWS, 1), F32)
     sums = scores(4, (nought, nought, nought), own=True)
+    tp[...] = jnp.zeros_like(tp)
 
     for p in range(PIECES):
         halo_wait(2, p)
@@ -221,28 +245,32 @@
         halo_wait(6, p)
         halo(6, 8, p, 5, behind)
         halo(6, 5 + 2 * core, p, 6, sibling)
-    sums = scores(2, sums)
-    sums = scores(6, sums)
+    x_wait(slot_rows(-1, core, 0), 1, 0)
+    x_copy(slot_rows(-1, core, 0), 5, 3, 0, right)
+    x_wait(slot_rows(1, core, 1), 2, 1)
+    x_copy(slot_rows(1, core, 1), 6, 3, 1, left)
     for slot in (5 - 2 * core, 3 - 2 * core, 7 - 2 * core):
         for p in range(PIECES):
             halo_wait(slot, p)
+
+    for i, (rows_slots, slot, step) in enumerate((((2, 3), 6, 2), ((6,), 2, -2), ((6,), 3, -1))):
+        for r, value in enumerate(cross(rows_slots, slot)):
+            tp[i, r : r + 1, :ROWS] = value
+        copy = remote(
+            tp.at[i], tpr.at[i], tp_send.at[i], tp_recv.at[i], (wrap(blk + step, blocks), grp)
+        )
+        copy.start()
+        sends.append(copy)
+    for slot in (2, 6, 3, 5):
         sums = scores(slot, sums)
-
-    x_wait(slot_rows(-1, core), 1, 0)
-    x_copy(slot_rows(-1, core, 0), 3, 3, 0, right)
-    x_copy(slot_rows(-1, core), 5, 4, 0, sibling)
-    x_wait(slot_rows(1, core), 2, 0)
-    x_copy(slot_rows(1, core, 1), 4, 3, 1, left)
-    x_copy(slot_rows(1, core), 6, 5, 0, sibling)
-
-    for p in range(PIECES):
-        halo_wait(8 - 8 * core, p)
-        halo(8 - 8 * core, 7 - 6 * core, p, 7, sibling)
-    sums = scores(8 - 8 * core, sums)
-    for slot in (8 * core, 1 + 6 * core):
-        for p in range(PIECES):
-            halo_wait(slot, p)
-        sums = scores(slot, sums)
+    near = (2, 6, 3, 5, 7 - 6 * core)
+    s, e = tile(near[4])
+    ex[near[4]] = e
+    sc[near[4]] = s
+    for i in range(3):
+        remote(tpr.at[i], tpr.at[i], tp_send.at[0], tp_recv.at[i], sibling).wait_recv()
+    apart = jnp.transpose(jnp.concatenate([tpr[0] + tpr[1] + tpr[2], jnp.zeros((120, 256), F32)], axis=0))
+    sums = [value + apart[:ROWS, r : r + 1] for r, value in enumerate(sums)]
 
     denom, possum, count = sums
     inv_count = 1.0 / jnp.maximum(count, 1.0)
@@ -253,7 +281,7 @@
     columns = jnp.where(lane == 0, own_a, jnp.where(lane == 1, own_c, own_loss))
     flat = jnp.transpose(jnp.concatenate([columns, jnp.zeros((64, 128), F32)], axis=0))
     st[4] = flat[:8]
-    loss_ref[...] = flat[2:3]
+    loss_ref[...] = flat[2, :ROWS]
     steps = (4, -4, 3, -3, 2, -2, 1, -1)
     for i, step in enumerate(steps):
         copy = remote(
@@ -262,42 +290,66 @@
         copy.start()
         sends.append(copy)
 
+    def pass_far(p):
+        halo_wait(8 - 8 * core, p)
+        halo(8 - 8 * core, 7 - 6 * core, p, 7, sibling)
+
+    pass_far(0)
+    pass_far(1)
+    x_wait(slot_rows(-1, core, 1), 1, 1)
+    x_copy(slot_rows(-1, core), 7, 4, 0, sibling)
+    x_wait(slot_rows(1, core, 0), 2, 0)
+    x_copy(slot_rows(1, core), 8, 5, 0, sibling)
+
+    def pairs(slot, s, e, own=False):
+        if not own:
+            remote(st.at[slot], st.at[slot], st_send.at[0], st_recv.at[slot], sibling).wait_recv()
+        row = st[slot]
+        same = same_label(slot, own)
+        value = e * (own_a + row[0:1, :ROWS]) - jnp.where(same, own_c + row[1:2, :ROWS], 0.0)
+        held = value.astype(BF16)
+        pr[slot] = held
+        return jnp.sum(held.astype(F32) * s, axis=1, keepdims=True)
+
+    along = pairs(4, sc[4], ex[4], own=True)
+    for slot in near:
+        along = along + pairs(slot, sc[slot], ex[slot])
+    for n in range(4):
+        columns = pl.ds(n * 256, 256)
+        total = jnp.dot(pr[4], win[4, :, columns], preferred_element_type=F32)
+        for slot in near:
+            total = total + jnp.dot(pr[slot], win[slot, :, columns], preferred_element_type=F32)
+        gu[:, columns] = total
+    pass_far(2)
+    pass_far(3)
+    far = (8 - 8 * core, 8 * core, 1 + 6 * core)
+    for i, slot in enumerate(far):
+        if i:
+            for p in range(PIECES):
+                halo_wait(slot, p)
+        s, e = tile(slot)
+        along = along + pairs(slot, s, e)
+    along = along * (1.0 / SCALE)
     for half in (0, 1):
         x_wait(slot_rows(2, core, half), 3, half)
-        x_copy(slot_rows(2, core, half), 7 + half, 6, half, sibling)
-
-    def pairs(slot, own=False):
-        row = st[slot]
-        same = same_label(slot, own)
-        value = ex[slot] * (own_a + row[0:1, :ROWS]) - jnp.where(same, own_c + row[1:2, :ROWS], 0.0)
-        pr[slot] = value.astype(BF16)
-
-    pairs(4, own=True)
-    for step in (1, -1, 2, -2, 3, -3, 4, -4):
-        slot = 4 + step
-        remote(st.at[slot], st.at[slot], st_send.at[0], st_recv.at[slot], sibling).wait_recv()
-        pairs(slot)
-
-    along = jnp.zeros((ROWS, 1), F32)
-    for n in range(4):
-        columns = pl.ds(n * 256, 256)
-        total = jnp.dot(pr[0], win[0, :, columns], preferred_element_type=F32)
-        for slot in range(1, SLOTS):
+    x_copy(slot_rows(2, core), 9, 6, 0, sibling)
+
+    for step in (2, 1, 3, 0):
+        x_to = wrap(x_me + step, NX)
+        columns = pl.ds(pl.multiple_of(x_to * 256, 256), 256)
+        total = gu[:, columns]
+        for slot in far:
             total = total + jnp.dot(pr[slot], win[slot, :, columns], preferred_element_type=F32)
-        gu[:, columns] = total
-        along = along + jnp.sum(zn[:, columns] * total, axis=1, keepdims=True)
-    for j in range(2 * NX):
-        columns = pl.ds(j * SLICE, SLICE)
-        gzs[j] = ((gu[:, columns] - zn[:, columns] * along) * rnorm).astype(BF16)
-    g_sends = []
-    for step in (2, 1, 3, 0):
+        grad = ((total - zn[:, columns] * along) * rnorm).astype(BF16)
+        for which in (0, 1):
+            gzs[x_to * 2 + which] = grad[:, which * SLICE : (which + 1) * SLICE]
         for which in (0, 1):
             if step == 0 and which == 0:
                 target, device = x_me * 2 + 1 - core, sibling
             elif step == 0:
                 continue
             else:
-                target, device = wrap(x_me + step, NX) * 2 + which, x_peer(step, which)
+                target, device = x_to * 2 + which, x_peer(step, which)
             copy = remote(
                 gzs.at[target], gzg.at[own_rows, :], g_send.at[2 * step + which], g_recv.at[own_x], device
             )
@@ -308,55 +360,42 @@
     x_wait(slot_rows(0, 1 - core), 0, 0)
     x_wait(slot_rows(-1, 1 - core), 4, 0)
     x_wait(slot_rows(1, 1 - core), 5, 0)
-    for half in (0, 1):
-        x_wait(slot_rows(2, 1 - core, half), 6, half)
+    x_wait(slot_rows(2, 1 - core), 6, 0)
     for step, which in ((0, 1 - core), (1, 0), (1, 1), (3, 0), (3, 1), (2, 0), (2, 1)):
         source = wrap(x_me + step, NX) * 2 + which
         rows = slot_rows(step, which)
         remote(gzs.at[0], gzg.at[rows, :], g_send.at[0], g_recv.at[source], sibling).wait_recv()
 
-    for n in range(E // 256):
-        columns = pl.ds(n * 256, 256)
-        piece = lax.dot_general(
-            gzg[...], embg[:, columns], (((0,), (0,)), ((), ())), preferred_element_type=F32
-        )
-        part[pl.ds(n * 256, 256), :] = jnp.transpose(piece).astype(YTYPE)
-
-    def y_rows(yl, which):
-        return pl.ds(yl * (2 * YROWS) + which * YROWS, YROWS)
-
     def y_self(yl, which):
         return jnp.logical_and(core == yh_me, jnp.logical_and(yl_me == yl, core == which))
 
-    def y_copy(yl, which):
+    def y_copy(yl, which, part_no):
+        rows = pl.ds(yl * (2 * YROWS) + which * YROWS + part_no * YPART, YPART)
         return remote(
-            part.at[y_rows(yl, which), :], yb.at[y_me], y_send.at[yl, which], y_recv.at[y_me],
+            part.at[rows, :], yb.at[part_no, y_me], y_send.at[part_no, yl, which], y_recv.at[part_no, y_me],
             ((yl * NZ + z_me) * 2 + which, x_me * NYH + core),
         )
 
-    for yl in range(NYL):
-        for which in (0, 1):
-            @pl.when(jnp.logical_not(y_self(yl, which)))
-            def _(yl=yl, which=which):
-                y_copy(yl, which).start()
-
-            @pl.when(y_self(yl, which))
-            def _(yl=yl, which=which):
-                yb[y_me] = part[y_rows(yl, which), :]
-
-    for src in range(NY):
-        @pl.when(jnp.logical_or(y_me != src, core != yh_me))
-        def _(src=src):
-            remote(yb.at[src], yb.at[src], y_send.at[0, 0], y_recv.at[src], sibling).wait_recv()
-
-    total = yb[0].astype(F32)
-    for src in range(1, NY):
-        total = total + yb[src].astype(F32)
-    ysum[0:YROWS, :] = total
-    ysum[YROWS:, :] = jnp.zeros((ZPAD, SLICE), F32)
-
-    for i in range(NZ):
-        zs[i] = ysum[i * ZROWS : i * ZROWS + ZPAD, :]
+    def y_start(yl, which):
+        @pl.when(jnp.logical_not(y_self(yl, which)))
+        def _():
+            for part_no in (0, 1):
+                y_copy(yl, which, part_no).start()
+
+        @pl.when(y_self(yl, which))
+        def _():
+            for part_no in (0, 1):
+                start = yl * (2 * YROWS) + which * YROWS + part_no * YPART
+                yb[part_no, y_me] = part[start : start + YPART, :]
+
+    grads = jnp.transpose(gzg[...])
+    started = 0
+    for n in range(E // 256):
+        piece = jnp.dot(grads, embg[:, n * 256 : (n + 1) * 256], preferred_element_type=F32)
+        part[n * 256 : (n + 1) * 256, :] = jnp.transpose(piece).astype(YTYPE)
+        while (started + 1) * YROWS <= (n + 1) * 256:
+            y_start(started // 2, started % 2)
+            started += 1
 
     def z_copy(i, which):
         return remote(
@@ -367,15 +406,32 @@
     def z_self(i, which):
         return jnp.logical_and(z_me == core * (NZ // 2) + i, core == which)
 
-    for i in range(NZ // 2):
-        for which in (0, 1):
-            @pl.when(jnp.logical_not(z_self(i, which)))
-            def _(i=i, which=which):
-                z_copy(i, which).start()
-
-            @pl.when(z_self(i, which))
-            def _(i=i, which=which):
-                zb[z_me] = zs[i * 2 + which]
+    for part_no in (0, 1):
+        for src in range(NY):
+            @pl.when(jnp.logical_or(y_me != src, core != yh_me))
+            def _(src=src):
+                remote(
+                    yb.at[part_no, src], yb.at[part_no, src],
+                    y_send.at[0, 0, 0], y_recv.at[part_no, src], sibling,
+                ).wait_recv()
+
+        total = yb[part_no, 0].astype(F32)
+        for src in range(1, NY):
+            total = total + yb[part_no, src].astype(F32)
+        ysum[...] = total
+        for i in range(part_no * (NZ // 4), (part_no + 1) * (NZ // 4)):
+            for which in (0, 1):
+                first = (i % (NZ // 4) * 2 + which) * ZROWS
+                for row in range(ZROWS):
+                    zs[i * 2 + which, row] = ysum[first + row : first + row + 1, :]
+
+                @pl.when(jnp.logical_not(z_self(i, which)))
+                def _(i=i, which=which):
+                    z_copy(i, which).start()
+
+                @pl.when(z_self(i, which))
+                def _(i=i, which=which):
+                    zb[z_me] = zs[i * 2 + which]
 
     for src in range(NZ):
         @pl.when(jnp.logical_or(z_me != src, core != z_core))
@@ -385,7 +441,8 @@
     total = zb[0]
     for src in range(1, NZ):
         total = total + zb[src]
-    head_ref[...] = total[:ZROWS, :]
+    for row in range(ZROWS):
+        head_ref[row : row + 1, :] = total[row]
 
     for copy in sends:
         copy.wait_send()
@@ -393,7 +450,8 @@
         for which in (0, 1):
             @pl.when(jnp.logical_not(y_self(yl, which)))
             def _(yl=yl, which=which):
-                y_copy(yl, which).wait_send()
+                for part_no in (0, 1):
+                    y_copy(yl, which, part_no).wait_send()
     for i in range(NZ // 2):
         for which in (0, 1):
             @pl.when(jnp.logical_not(z_self(i, which)))
@@ -401,12 +459,21 @@
                 z_copy(i, which).wait_send()
 
 
+def hand_out(loss_in, head_in, loss_out, head_out, sem):
+    first = pltpu.make_async_copy(loss_in, loss_out, sem.at[0])
+    second = pltpu.make_async_copy(head_in, head_out, sem.at[1])
+    first.start()
+    second.start()
+    first.wait()
+    second.wait()
+
+
 def on_device(embeddings, proj_weight, labels, flags):
     dma = pltpu.SemaphoreType.DMA
     loss, head = pl.pallas_call(
         kernel,
         out_shape=(
-            jax.ShapeDtypeStruct((1, 256), F32),
+            jax.ShapeDtypeStruct((ROWS,), F32),
             jax.ShapeDtypeStruct((ZROWS, SLICE), F32),
         ),
         in_specs=[pl.BlockSpec(memory_space=pl.ANY)] * 4,
@@ -423,27 +490,32 @@
             pltpu.VMEM((ROWS, WIDTH), F32),
             pltpu.VMEM((SLOTS, ROWS, WIDTH), BF16),
             pltpu.VMEM((SLOTS, ROWS, ROWS), F32),
+            pltpu.VMEM((SLOTS, ROWS, ROWS), F32),
             pltpu.VMEM((SLOTS, ROWS, ROWS), BF16),
             pltpu.VMEM((SLOTS, 8, 256), F32),
+            pltpu.VMEM((3, 8, 256), F32),
+            pltpu.VMEM((3, 8, 256), F32),
             pltpu.VMEM((ROWS, WIDTH), F32),
             pltpu.VMEM((2 * NX, ROWS, SLICE), BF16),
             pltpu.VMEM((2 * NX * ROWS, SLICE), BF16),
             pltpu.VMEM((E, SLICE), YTYPE),
-            pltpu.VMEM((NY, YROWS, SLICE), YTYPE),
-            pltpu.VMEM((YROWS + ZPAD, SLICE), F32),
-            pltpu.VMEM((NZ, ZPAD, SLICE), F32),
-            pltpu.VMEM((NZ, ZPAD, SLICE), F32),
+            pltpu.VMEM((2, NY, YPART, SLICE), YTYPE),
+            pltpu.VMEM((YPART, SLICE), F32),
+            pltpu.VMEM((NZ, ZROWS, 1, SLICE), F32),
+            pltpu.VMEM((NZ, ZROWS, 1, SLICE), F32),
             dma((7,)),
             dma((8, PIECES)),
             dma((SLOTS, PIECES)),
-            dma((9,)),
+            dma((10,)),
             dma((7, 2)),
             dma((8,)),
             dma((SLOTS,)),
+            dma((3,)),
+            dma((3,)),
             dma((8,)),
             dma((2 * NX,)),
-            dma((NYL, 2)),
-            dma((NY,)),
+            dma((2, NYL, 2)),
+            dma((2, NY)),
             dma((NZ // 2, 2)),
             dma((NZ,)),
         ],
@@ -452,7 +524,18 @@
         ),
         name="contrastive_loss_and_head_gradient",
     )(embeddings, proj_weight, labels.reshape(1536, 128), flags.reshape(1536, 128))
-    return loss[0, :ROWS], head
+    return pl.pallas_call(
+        hand_out,
+        out_shape=(
+            jax.ShapeDtypeStruct((ROWS,), F32),
+            jax.ShapeDtypeStruct((ZROWS, SLICE), F32),
+        ),
+        in_specs=[pl.BlockSpec(memory_space=pl.ANY)] * 2,
+        out_specs=(pl.BlockSpec(memory_space=pl.ANY), pl.BlockSpec(memory_space=pl.ANY)),
+        scratch_shapes=[dma((2,))],
+        compiler_params=pltpu.CompilerParams(vmem_limit_bytes=60 * 2**20),
+        name="hand_out",
+    )(loss, head)
 
 
 def solution(mesh):

time: 84.8 us -> 75.2 us (0.89)
  the two profiles are of different devices: /device:TPU:81 before, /device:TPU:17 now
where the time goes in v2:
time: 75.2 us; the launch traced here: 75.1 us
  Pallas kernels  74.4 us (99%)
    pallas_call x1, Pallas kernels, on_device(): pl.pallas_call(kernel, out_shape=(jax.ShapeDtypeStruct((ROWS,), F32), jax...  73.1 us

profile of v2, /device:TPU:17, one launch (start us, length us, event | category | flops | bytes accessed | tf_op | source)
XLA Modules:
  0.0 75.1 jit_solution(13019464907813473597)
XLA Ops:
  0.6 73.1 %contrastive_loss_and_head_gradient.1 = (f32[192]{0:T(256)}, f32[10,128]{1,0:T(8,128)}) custom-call(bf16[192,1280]{1,0:T(8,128)(2,1)} %emb_hbm.1, bf16[1280,1024]{1,0:T(8,128)(2,1)} %w_hbm.1, s32[1536,128]{1,0:T(8,128)} %bitcast.2, s32[1536,128]{1,0:T(8,128)} %bitcast.3), custom_call_target="tpu_custom_call" | custom-call | tf_op jit(solution)/shard_map/contrastive_loss_and_head_gradient/pallas_call | solution.py:473
  73.8 1.3 %hand_out.1 = (f32[192]{0:T(256)}, f32[10,128]{1,0:T(8,128)}) custom-call(f32[192]{0:T(256)} %get-tuple-element.4.loss_in, f32[10,128]{1,0:T(8,128)} %get-tuple-element.5.head_in), custom_call_target="tpu_custom_call" | custom-call | tf_op jit(solution)/shard_map/hand_out/pallas_call | solution.py:527

commit v3 on v2

v3 whole, which is shorter than its diff:
```python
import functools

import jax
import jax.numpy as jnp
from jax import lax
from jax.experimental import pallas as pl
from jax.experimental.pallas import tpu as pltpu
from jax.sharding import PartitionSpec as P

MESH = pl.DeviceIdType.MESH
F32 = jnp.float32
BF16 = jnp.bfloat16

NX, NYH, NYL, NZ = 4, 2, 4, 16
NY = NYH * NYL
ROWS, E, WIDTH = 192, 1280, 1024
SLOTS = 9
LABEL_ROWS = 1536
PIECES = 4
PIECE = ROWS // PIECES
HALFROWS = ROWS // 2
SLICE = 128
YROWS = E // NYL // 2
YPART = YROWS // 2
ZROWS = 10
SCALE = 10.0
YTYPE = BF16


def kernel(
    emb_hbm, w_hbm, lab_hbm, flag_hbm, loss_ref, head_ref,
    w_v, lab_v, lw, embg, zn, win, ex, sc, pr, st, gzs, gzg, part, yb, ysum, zs, zb,
    load_sem, halo_send, halo_recv, halo_whole, x_send, x_recv, st_send, st_recv,
    g_send, g_recv, y_send, y_recv, z_send, z_recv,
):
    blk = lax.axis_index("blk")
    grp = lax.axis_index("grp")
    blocks = 2 * NYL * NZ
    core = lax.rem(blk, 2)
    chip = blk // 2
    z_me = lax.rem(chip, NZ)
    yl_me = chip // NZ
    x_me = grp // NYH
    yh_me = lax.rem(grp, NYH)
    y_me = yh_me * NYL + yl_me
    own_x = x_me * 2 + core

    def wrap(value, size):
        return lax.rem(value + size, size)

    def chip_peer(step, which):
        return wrap(chip + step, blocks // 2) * 2 + which, grp

    def x_peer(step, which):
        return chip * 2 + which, wrap(x_me + step, NX) * NYH + yh_me

    sibling = (chip * 2 + 1 - core, grp)
    z_core = z_me // (NZ // 2)

    def remote(src, dst, send, recv, device):
        return pltpu.make_async_remote_copy(
            src_ref=src, dst_ref=dst, send_sem=send, recv_sem=recv, device_id=device, device_id_type=MESH
        )

    own_rows = pl.ds(pl.multiple_of(own_x * ROWS, 16), ROWS)
    loads = [pltpu.make_async_copy(emb_hbm, embg.at[own_rows, :], load_sem.at[0])]
    for n in range(4):
        columns = pl.ds(n * 256, 256)
        loads.append(pltpu.make_async_copy(w_hbm.at[:, columns], w_v.at[:, columns], load_sem.at[1 + n]))

    def label_start(block):
        row = block * 12 + (3 * grp) // 2
        first = jnp.minimum(row - lax.rem(row, 8), LABEL_ROWS - 16)
        return pl.multiple_of(first, 8), row - first

    for slot in range(SLOTS):
        rows = pl.ds(label_start(wrap(blk + slot - 4, blocks))[0], 16)
        loads.append(pltpu.make_async_copy(lab_hbm.at[rows, :], lab_v.at[slot], load_sem.at[5 + slot]))
    rows = pl.ds(label_start(blk)[0], 16)
    loads.append(pltpu.make_async_copy(flag_hbm.at[rows, :], lab_v.at[SLOTS], load_sem.at[5 + SLOTS]))
    for load in loads:
        load.start()

    barrier = pltpu.get_barrier_semaphore()

    def greet(device):
        pl.semaphore_signal(barrier, inc=1, device_id=device, device_id_type=MESH)

    for step in (1, -1, 2, -2, 3, -3, 4, -4):
        greet((wrap(blk + step, blocks), grp))
    for step in (1, 2, 3):
        for which in (0, 1):
            greet(x_peer(step, which))

    def greet_y(y_src, carry):
        @pl.when(jnp.logical_or(y_src != y_me, core != yh_me))
        def _():
            greet(((lax.rem(y_src, NYL) * NZ + z_me) * 2 + yh_me, x_me * NYH + y_src // NYL))
        return carry

    lax.fori_loop(0, NY, greet_y, 0)

    def greet_z(z_src, carry):
        @pl.when(jnp.logical_or(z_src != z_me, core != z_core))
        def _():
            greet(((yl_me * NZ + z_src) * 2 + z_core, grp))
        return carry

    lax.fori_loop(0, NZ, greet_z, 0)

    loads[0].wait()
    greeted = (
        8 + 6 + NY + NZ
        - jnp.where(core == yh_me, 1, 0).astype(jnp.int32)
        - jnp.where(core == z_core, 1, 0).astype(jnp.int32)
    )
    ahead, behind = chip_peer(1, core), chip_peer(-1, core)

    def halo_sem(slot, p):
        if isinstance(slot, int) and slot in (0, 2, 6, 8):
            return halo_recv.at[slot // 2, p]
        return halo_whole.at[slot]

    def halo(src_slot, dst_slot, p, device):
        rows = pl.ds(p * PIECE, PIECE)
        remote(
            win.at[src_slot, rows, :], win.at[dst_slot, rows, :],
            halo_send, halo_sem(dst_slot, p), device,
        ).start()

    def halo_wait(slot, p):
        rows = pl.ds(p * PIECE, PIECE)
        remote(win.at[slot, rows, :], win.at[slot, rows, :], halo_send, halo_sem(slot, p), sibling).wait_recv()

    def halo_wait_all(slot):
        remote(win.at[slot], win.at[slot], halo_send, halo_whole.at[slot], sibling).wait_recv()

    rnorms = []
    for half in (0, 1):
        rows = slice(half * HALFROWS, (half + 1) * HALFROWS)
        emb = embg[pl.ds(pl.multiple_of(own_x * ROWS + half * HALFROWS, 16), HALFROWS), :]
        ssq = jnp.zeros((HALFROWS, 1), F32)
        for n in range(4):
            columns = pl.ds(n * 256, 256)
            if half == 0:
                loads[1 + n].wait()
            zc = jnp.dot(emb, w_v[:, columns], preferred_element_type=F32)
            zn[rows, columns] = zc
            ssq = ssq + jnp.sum(zc * zc, axis=1, keepdims=True)
        rnorms.append(1.0 / jnp.sqrt(ssq + 1e-6))
        for n in range(4):
            columns = pl.ds(n * 256, 256)
            zc = zn[rows, columns] * rnorms[half]
            zn[rows, columns] = zc
            win[4, rows, columns] = zc.astype(BF16)
        if half == 0:
            pl.semaphore_wait(barrier, greeted)
        for p in range(half * (PIECES // 2), (half + 1) * (PIECES // 2)):
            halo(4, 2, p, ahead)
            halo(4, 6, p, behind)
            halo(4, 3 + 2 * core, p, sibling)
    rnorm = jnp.concatenate(rnorms, axis=0)

    right, left = x_peer(1, core), x_peer(-1, core)

    def slot_rows(x_step, which, half=None):
        start = (wrap(x_me + x_step, NX) * 2 + which) * ROWS
        if half is None:
            return pl.ds(pl.multiple_of(start, 16), ROWS)
        return pl.ds(pl.multiple_of(start + half * HALFROWS, 16), HALFROWS)

    def x_copy(rows, recv, half, device):
        remote(embg.at[rows, :], embg.at[rows, :], x_send, x_recv.at[recv, half], device).start()

    def x_wait(rows, recv, half):
        remote(embg.at[rows, :], embg.at[rows, :], x_send, x_recv.at[recv, half], sibling).wait_recv()

    x_copy(own_rows, 0, 0, sibling)
    for half in (0, 1):
        x_copy(slot_rows(0, core, half), 1, half, right)
    for half in (1, 0):
        x_copy(slot_rows(0, core, half), 2, half, left)

    for load in loads[5:]:
        load.wait()
    odd = lax.rem(grp, 2) == 1

    lw[...] = jnp.zeros_like(lw)
    for slot in range(SLOTS + 1):
        offset = label_start(wrap(blk + slot - 4, blocks) if slot < SLOTS else blk)[1]
        lw[slot : slot + 1, 0:128] = lab_v[slot, pl.ds(offset, 1), :].astype(F32)
        lw[slot : slot + 1, 128:256] = lab_v[slot, pl.ds(offset + 1, 1), :].astype(F32)
    plain = lw[...]
    lw[...] = jnp.where(odd, pltpu.roll(plain, 192, 1), plain)
    turned = jnp.transpose(jnp.concatenate([lw[...], jnp.zeros((112, 256), F32)], axis=0))
    own_lab = turned[:ROWS, 4:5]
    own_w = jnp.where(turned[:ROWS, SLOTS : SLOTS + 1] == 1.0, 0.5, 1.0)
    diagonal = lax.broadcasted_iota(jnp.int32, (ROWS, ROWS), 0) == lax.broadcasted_iota(
        jnp.int32, (ROWS, ROWS), 1
    )

    def same_label(slot, own):
        same = own_lab == lw[pl.ds(slot, 1), :ROWS]
        return jnp.logical_and(same, jnp.logical_not(diagonal)) if own else same

    own_unit = win[4]

    def scores(slot, sums, own=False):
        denom, possum, count = sums
        s = SCALE * lax.dot_general(
            own_unit, win[slot], (((1,), (1,)), ((), ())), preferred_element_type=F32
        )
        e = jnp.exp(s)
        if own:
            e = jnp.where(diagonal, 0.0, e)
        same = same_label(slot, own)
        ex[slot] = e
        sc[slot] = s
        denom = denom + jnp.sum(e, axis=1, keepdims=True)
        possum = possum + jnp.sum(jnp.where(same, s, 0.0), axis=1, keepdims=True)
        count = count + jnp.sum(jnp.where(same, 1.0, 0.0), axis=1, keepdims=True)
        return denom, possum, count

    nought = jnp.zeros((ROWS, 1), F32)
    sums = scores(4, (nought, nought, nought), own=True)

    for p in range(PIECES):
        halo_wait(2, p)
        halo(2, 0, p, ahead)
        halo(2, 1 + 2 * core, p, sibling)
        halo_wait(6, p)
        halo(6, 8, p, behind)
        halo(6, 5 + 2 * core, p, sibling)
    x_wait(slot_rows(-1, core, 0), 1, 0)
    x_copy(slot_rows(-1, core, 0), 3, 0, right)
    x_wait(slot_rows(1, core, 1), 2, 1)
    x_copy(slot_rows(1, core, 1), 3, 1, left)
    sums = scores(2, sums)
    sums = scores(6, sums)
    for slot in (5 - 2 * core, 3 - 2 * core, 7 - 2 * core):
        halo_wait_all(slot)
        sums = scores(slot, sums)

    @pl.when(core == 0)
    def _():
        for p in range(PIECES):
            halo_wait(8, p)
            halo(8, 7, p, sibling)
        for p in range(PIECES):
            halo_wait(0, p)

    @pl.when(core == 1)
    def _():
        for p in range(PIECES):
            halo_wait(0, p)
            halo(0, 1, p, sibling)
        for p in range(PIECES):
            halo_wait(8, p)

    sums = scores(0, sums)
    sums = scores(8, sums)
    halo_wait_all(1 + 6 * core)
    sums = scores(1 + 6 * core, sums)

    denom, possum, count = sums
    inv_count = 1.0 / jnp.maximum(count, 1.0)
    own_loss = own_w * (jnp.log(denom) - possum * inv_count)
    own_a = (SCALE * own_w) / denom
    own_c = (SCALE * own_w) * inv_count
    lane = lax.broadcasted_iota(jnp.int32, (ROWS, 128), 1)
    columns = jnp.where(lane == 0, own_a, jnp.where(lane == 1, own_c, own_loss))
    flat = jnp.transpose(jnp.concatenate([columns, jnp.zeros((64, 128), F32)], axis=0))
    st[4] = flat[:8]
    loss_ref[...] = flat[2, :ROWS]
    for step in (4, -4, 3, -3, 2, -2, 1, -1):
        remote(st.at[4], st.at[4 - step], st_send, st_recv, (wrap(blk + step, blocks), grp)).start()

    x_wait(slot_rows(-1, core, 1), 1, 1)
    x_copy(slot_rows(-1, core), 4, 0, sibling)
    x_wait(slot_rows(1, core, 0), 2, 0)
    x_copy(slot_rows(1, core), 5, 0, sibling)
    for half in (0, 1):
        x_wait(slot_rows(2, core, half), 3, half)
    x_copy(slot_rows(2, core), 6, 0, sibling)

    def pairs(slot, own=False):
        row = st[slot]
        same = same_label(slot, own)
        value = ex[slot] * (own_a + row[0:1, :ROWS]) - jnp.where(same, own_c + row[1:2, :ROWS], 0.0)
        held = value.astype(BF16)
        pr[slot] = held
        return jnp.sum(held.astype(F32) * sc[slot], axis=1, keepdims=True)

    along = pairs(4, own=True)
    remote(st.at[0:8], st.at[0:8], st_send, st_recv, sibling).wait_recv()
    for slot in (0, 1, 2, 3, 5, 6, 7, 8):
        along = along + pairs(slot)
    along = along * (1.0 / SCALE)

    for step in (2, 1, 3, 0):
        x_to = wrap(x_me + step, NX)
        columns = pl.ds(pl.multiple_of(x_to * 256, 256), 256)
        total = jnp.dot(pr[0], win[0, :, columns], preferred_element_type=F32)
        for slot in range(1, SLOTS):
            total = total + jnp.dot(pr[slot], win[slot, :, columns], preferred_element_type=F32)
        grad = ((total - zn[:, columns] * along) * rnorm).astype(BF16)
        for which in (0, 1):
            gzs[x_to * 2 + which] = grad[:, which * SLICE : (which + 1) * SLICE]
        for which in (0, 1):
            if step == 0 and which == 0:
                target, device = x_me * 2 + 1 - core, sibling
            elif step == 0:
                continue
            else:
                target, device = x_to * 2 + which, x_peer(step, which)
            remote(gzs.at[target], gzg.at[own_rows, :], g_send, g_recv, device).start()
    gzg[own_rows, :] = gzs[own_x]

    x_wait(slot_rows(0, 1 - core), 0, 0)
    x_wait(slot_rows(-1, 1 - core), 4, 0)
    x_wait(slot_rows(1, 1 - core), 5, 0)
    x_wait(slot_rows(2, 1 - core), 6, 0)
    remote(gzs.at[0:7], gzs.at[0:7], g_send, g_recv, sibling).wait_recv()

    def y_self(yl, which):
        return jnp.logical_and(core == yh_me, jnp.logical_and(yl_me == yl, core == which))

    def y_copy(yl, which, part_no):
        rows = pl.ds(yl * (2 * YROWS) + which * YROWS + part_no * YPART, YPART)
        return remote(
            part.at[rows, :], yb.at[part_no, y_me], y_send, y_recv.at[part_no],
            ((yl * NZ + z_me) * 2 + which, x_me * NYH + core),
        )

    def y_start(yl, which):
        @pl.when(jnp.logical_not(y_self(yl, which)))
        def _():
            for part_no in (0, 1):
                y_copy(yl, which, part_no).start()

        @pl.when(y_self(yl, which))
        def _():
            for part_no in (0, 1):
                start = yl * (2 * YROWS) + which * YROWS + part_no * YPART
                yb[part_no, y_me] = part[start : start + YPART, :]

    grads = jnp.transpose(gzg[...])
    started = 0
    for n in range(E // 256):
        piece = jnp.dot(grads, embg[:, n * 256 : (n + 1) * 256], preferred_element_type=F32)
        part[n * 256 : (n + 1) * 256, :] = jnp.transpose(piece).astype(YTYPE)
        while (started + 1) * YROWS <= (n + 1) * 256:
            y_start(started // 2, started % 2)
            started += 1

    def z_copy(i, which):
        return remote(
            zs.at[i * 2 + which], zb.at[z_me], z_send, z_recv,
            ((yl_me * NZ + core * (NZ // 2) + i) * 2 + which, grp),
        )

    def z_self(i, which):
        return jnp.logical_and(z_me == core * (NZ // 2) + i, core == which)

    def y_wait(pieces, part_no):
        rows = yb.at[part_no, 0:pieces]
        remote(rows, rows, y_send, y_recv.at[part_no], sibling).wait_recv()

    for part_no in (0, 1):
        @pl.when(core == yh_me)
        def _(part_no=part_no):
            y_wait(NY - 1, part_no)

        @pl.when(core != yh_me)
        def _(part_no=part_no):
            y_wait(NY, part_no)

        total = yb[part_no, 0].astype(F32)
        for src in range(1, NY):
            total = total + yb[part_no, src].astype(F32)
        ysum[...] = total
        for i in range(part_no * (NZ // 4), (part_no + 1) * (NZ // 4)):
            for which in (0, 1):
                first = (i % (NZ // 4) * 2 + which) * ZROWS
                for row in range(ZROWS):
                    zs[i * 2 + which, row] = ysum[first + row : first + row + 1, :]

                @pl.when(jnp.logical_not(z_self(i, which)))
                def _(i=i, which=which):
                    z_copy(i, which).start()

                @pl.when(z_self(i, which))
                def _(i=i, which=which):
                    zb[z_me] = zs[i * 2 + which]

    @pl.when(core == z_core)
    def _():
        remote(zb.at[1:NZ], zb.at[1:NZ], z_send, z_recv, sibling).wait_recv()

    @pl.when(core != z_core)
    def _():
        remote(zb, zb, z_send, z_recv, sibling).wait_recv()

    total = zb[0]
    for src in range(1, NZ):
        total = total + zb[src]
    for row in range(ZROWS):
        head_ref[row : row + 1, :] = total[row]

    remote(win.at[0:8], win.at[0:8], halo_send, halo_whole.at[0], sibling).wait_send()
    remote(embg.at[0 : 7 * ROWS, :], embg.at[0 : 7 * ROWS, :], x_send, x_recv.at[0, 0], sibling).wait_send()
    remote(st.at[0:8], st.at[0:8], st_send, st_recv, sibling).wait_send()
    remote(gzs.at[0:7], gzs.at[0:7], g_send, g_recv, sibling).wait_send()

    @pl.when(core == yh_me)
    def _():
        remote(yb.at[:, 1:NY], yb.at[:, 1:NY], y_send, y_recv.at[0], sibling).wait_send()

    @pl.when(core != yh_me)
    def _():
        remote(yb, yb, y_send, y_recv.at[0], sibling).wait_send()

    @pl.when(core == z_core)
    def _():
        remote(zs.at[1:NZ], zs.at[1:NZ], z_send, z_recv, sibling).wait_send()

    @pl.when(core != z_core)
    def _():
        remote(zs, zs, z_send, z_recv, sibling).wait_send()


def hand_out(loss_in, head_in, loss_out, head_out, sem):
    first = pltpu.make_async_copy(loss_in, loss_out, sem.at[0])
    second = pltpu.make_async_copy(head_in, head_out, sem.at[1])
    first.start()
    second.start()
    first.wait()
    second.wait()


def on_device(embeddings, proj_weight, labels, flags):
    dma = pltpu.SemaphoreType.DMA
    loss, head = pl.pallas_call(
        kernel,
        out_shape=(
            jax.ShapeDtypeStruct((ROWS,), F32),
            jax.ShapeDtypeStruct((ZROWS, SLICE), F32),
        ),
        in_specs=[pl.BlockSpec(memory_space=pl.ANY)] * 4,
        out_specs=(
            pl.BlockSpec(memory_space=pltpu.VMEM),
            pl.BlockSpec(memory_space=pltpu.VMEM),
        ),
        scratch_shapes=[
            pltpu.VMEM((E, WIDTH), BF16),
            pltpu.VMEM((SLOTS + 1, 16, 128), jnp.int32),
            pltpu.VMEM((16, 256), F32),
            pltpu.VMEM((2 * NX * ROWS, E), BF16),
            pltpu.VMEM((ROWS, WIDTH), F32),
            pltpu.VMEM((SLOTS, ROWS, WIDTH), BF16),
            pltpu.VMEM((SLOTS, ROWS, ROWS), F32),
            pltpu.VMEM((SLOTS, ROWS, ROWS), F32),
            pltpu.VMEM((SLOTS, ROWS, ROWS), BF16),
            pltpu.VMEM((SLOTS, 8, 256), F32),
            pltpu.VMEM((2 * NX, ROWS, SLICE), BF16),
            pltpu.VMEM((2 * NX * ROWS, SLICE), BF16),
            pltpu.VMEM((E, SLICE), YTYPE),
            pltpu.VMEM((2, NY, YPART, SLICE), YTYPE),
            pltpu.VMEM((YPART, SLICE), F32),
            pltpu.VMEM((NZ, ZROWS, 1, SLICE), F32),
            pltpu.VMEM((NZ, ZROWS, 1, SLICE), F32),
            dma((15,)),
            dma,
            dma((5, PIECES)),
            dma((SLOTS,)),
            dma,
            dma((7, 2)),
            dma,
            dma,
            dma,
            dma,
            dma,
            dma((2,)),
            dma,
            dma,
        ],
        compiler_params=pltpu.CompilerParams(
            collective_id=0, has_side_effects=True, vmem_limit_bytes=60 * 2**20
        ),
        name="contrastive_loss_and_head_gradient",
    )(embeddings, proj_weight, labels.reshape(LABEL_ROWS, 128), flags.reshape(LABEL_ROWS, 128))
    return pl.pallas_call(
        hand_out,
        out_shape=(
            jax.ShapeDtypeStruct((ROWS,), F32),
            jax.ShapeDtypeStruct((ZROWS, SLICE), F32),
        ),
        in_specs=[pl.BlockSpec(memory_space=pl.ANY)] * 2,
        out_specs=(pl.BlockSpec(memory_space=pl.ANY), pl.BlockSpec(memory_space=pl.ANY)),
        scratch_shapes=[dma((2,))],
        compiler_params=pltpu.CompilerParams(vmem_limit_bytes=60 * 2**20),
        name="hand_out",
    )(loss, head)


def solution(mesh):
    return jax.shard_map(
        on_device,
        mesh=mesh,
        in_specs=(P(("blk", "grp"), None), P(), P(), P()),
        out_specs=(P(("blk", "grp")), P("blk", "grp")),
        check_vma=False,
    )
```

time: 75.2 us -> 72.6 us (0.965)
  the two profiles are of different devices: /device:TPU:17 before, /device:TPU:81 now
where the time goes in v3:
time: 72.6 us; the launch traced here: 72.5 us
  Pallas kernels  71.8 us (99%)
    pallas_call x1, Pallas kernels, on_device(): pl.pallas_call(kernel, out_shape=(jax.ShapeDtypeStruct((ROWS,), F32), jax...  70.5 us

profile of v3, /device:TPU:81, one launch (start us, length us, event | category | flops | bytes accessed | tf_op | source)
XLA Modules:
  0.0 72.5 jit_solution(15893832741022858481)
XLA Ops:
  0.6 70.5 %contrastive_loss_and_head_gradient.1 = (f32[192]{0:T(256)}, f32[10,128]{1,0:T(8,128)}) custom-call(bf16[192,1280]{1,0:T(8,128)(2,1)} %emb_hbm.1, bf16[1280,1024]{1,0:T(8,128)(2,1)} %w_hbm.1, s32[1536,128]{1,0:T(8,128)} %bitcast.2, s32[1536,128]{1,0:T(8,128)} %bitcast.3), custom_call_target="tpu_custom_call" | custom-call | tf_op jit(solution)/shard_map/contrastive_loss_and_head_gradient/pallas_call | solution.py:443
  71.1 1.3 %hand_out.1 = (f32[192]{0:T(256)}, f32[10,128]{1,0:T(8,128)}) custom-call(f32[192]{0:T(256)} %get-tuple-element.4.loss_in, f32[10,128]{1,0:T(8,128)} %get-tuple-element.5.head_in), custom_call_target="tpu_custom_call" | custom-call | tf_op jit(solution)/shard_map/hand_out/pallas_call | solution.py:492

commit v4 on v3

--- a/solution.py
+++ b/solution.py
@@ -332,17 +332,15 @@
             ((yl * NZ + z_me) * 2 + which, x_me * NYH + core),
         )
 
-    def y_start(yl, which):
+    def y_start(yl, which, part_no):
         @pl.when(jnp.logical_not(y_self(yl, which)))
         def _():
-            for part_no in (0, 1):
-                y_copy(yl, which, part_no).start()
+            y_copy(yl, which, part_no).start()
 
         @pl.when(y_self(yl, which))
         def _():
-            for part_no in (0, 1):
-                start = yl * (2 * YROWS) + which * YROWS + part_no * YPART
-                yb[part_no, y_me] = part[start : start + YPART, :]
+            start = yl * (2 * YROWS) + which * YROWS + part_no * YPART
+            yb[part_no, y_me] = part[start : start + YPART, :]
 
     grads = jnp.transpose(gzg[...])
     started = 0
@@ -350,8 +348,10 @@
         piece = jnp.dot(grads, embg[:, n * 256 : (n + 1) * 256], preferred_element_type=F32)
         part[n * 256 : (n + 1) * 256, :] = jnp.transpose(piece).astype(YTYPE)
         while (started + 1) * YROWS <= (n + 1) * 256:
-            y_start(started // 2, started % 2)
+            y_start(started // 2, started % 2, 0)
             started += 1
+    for i in range(2 * NYL):
+        y_start(i // 2, i % 2, 1)
 
     def z_copy(i, which):
         return remote(
@@ -442,10 +442,7 @@
     dma = pltpu.SemaphoreType.DMA
     loss, head = pl.pallas_call(
         kernel,
-        out_shape=(
-            jax.ShapeDtypeStruct((ROWS,), F32),
-            jax.ShapeDtypeStruct((ZROWS, SLICE), F32),
-        ),
+        out_shape=(pltpu.VMEM((ROWS,), F32), pltpu.VMEM((ZROWS, SLICE), F32)),
         in_specs=[pl.BlockSpec(memory_space=pl.ANY)] * 4,
         out_specs=(
             pl.BlockSpec(memory_space=pltpu.VMEM),
@@ -495,10 +492,10 @@
             jax.ShapeDtypeStruct((ROWS,), F32),
             jax.ShapeDtypeStruct((ZROWS, SLICE), F32),
         ),
-        in_specs=[pl.BlockSpec(memory_space=pl.ANY)] * 2,
+        in_specs=[pl.BlockSpec(memory_space=pltpu.VMEM)] * 2,
         out_specs=(pl.BlockSpec(memory_space=pl.ANY), pl.BlockSpec(memory_space=pl.ANY)),
         scratch_shapes=[dma((2,))],
-        compiler_params=pltpu.CompilerParams(vmem_limit_bytes=60 * 2**20),
+        compiler_params=pltpu.CompilerParams(vmem_limit_bytes=2**20),
         name="hand_out",
     )(loss, head)
 

time: 72.6 us -> 69.5 us (0.957)
  the two profiles are of different devices: /device:TPU:81 before, /device:TPU:17 now
where the time goes in v4:
time: 69.5 us; the launch traced here: 69.3 us
  Pallas kernels  68.7 us (99%)
    pallas_call x1, Pallas kernels, on_device(): pl.pallas_call(kernel, out_shape=(pltpu.VMEM((ROWS,), F32), pltpu.VMEM((Z...  68.1 us

profile of v4, /device:TPU:17, one launch (start us, length us, event | category | flops | bytes accessed | tf_op | source)
XLA Modules:
  0.0 69.3 jit_solution(6118486079457818376)
XLA Ops:
  0.6 68.1 %contrastive_loss_and_head_gradient.1 = (f32[192]{0:T(256)S(1)}, f32[10,128]{1,0:T(8,128)S(1)}) custom-call(bf16[192,1280]{1,0:T(8,128)(2,1)} %emb_hbm.1, bf16[1280,1024]{1,0:T(8,128)(2,1)} %w_hbm.1, s32[1536,128]{1,0:T(8,128)} %bitcast.2, s32[1536,128]{1,0:T(8,128)} %bitcast.3), custom_call_target="tpu_custom_call" | custom-call | tf_op jit(solution)/shard_map/contrastive_loss_and_head_gradient/pallas_call | solution.py:443
  68.7 0.6 hand_out.1

commit v5 on v4

--- a/solution.py
+++ b/solution.py
@@ -67,6 +67,32 @@
     for n in range(4):
         columns = pl.ds(n * 256, 256)
         loads.append(pltpu.make_async_copy(w_hbm.at[:, columns], w_v.at[:, columns], load_sem.at[1 + n]))
+    for load in loads:
+        load.start()
+
+    barrier = pltpu.get_barrier_semaphore()
+
+    def greet(device):
+        pl.semaphore_signal(barrier, inc=1, device_id=device, device_id_type=MESH)
+
+    for step in (8, 7, 9, 6, 10, 5, 11, 4, 12, 3, 13, 2, 14, 1, 15):
+        greet(((yl_me * NZ + wrap(z_me + step, NZ)) * 2 + z_core, grp))
+    for step in (4, 3, 5, 2, 6, 1, 7):
+        y_src = wrap(y_me + step, NY)
+        greet(((lax.rem(y_src, NYL) * NZ + z_me) * 2 + yh_me, x_me * NYH + y_src // NYL))
+    for step in (2, 1, 3):
+        for which in (0, 1):
+            greet(x_peer(step, which))
+    for step in (4, -4, 3, -3, 2, -2, 1, -1):
+        greet((wrap(blk + step, blocks), grp))
+
+    @pl.when(core != z_core)
+    def _():
+        greet(sibling)
+
+    @pl.when(core != yh_me)
+    def _():
+        greet(sibling)
 
     def label_start(block):
         row = block * 12 + (3 * grp) // 2
@@ -78,35 +104,8 @@
         loads.append(pltpu.make_async_copy(lab_hbm.at[rows, :], lab_v.at[slot], load_sem.at[5 + slot]))
     rows = pl.ds(label_start(blk)[0], 16)
     loads.append(pltpu.make_async_copy(flag_hbm.at[rows, :], lab_v.at[SLOTS], load_sem.at[5 + SLOTS]))
-    for load in loads:
+    for load in loads[5:]:
         load.start()
-
-    barrier = pltpu.get_barrier_semaphore()
-
-    def greet(device):
-        pl.semaphore_signal(barrier, inc=1, device_id=device, device_id_type=MESH)
-
-    for step in (1, -1, 2, -2, 3, -3, 4, -4):
-        greet((wrap(blk + step, blocks), grp))
-    for step in (1, 2, 3):
-        for which in (0, 1):
-            greet(x_peer(step, which))
-
-    def greet_y(y_src, carry):
-        @pl.when(jnp.logical_or(y_src != y_me, core != yh_me))
-        def _():
-            greet(((lax.rem(y_src, NYL) * NZ + z_me) * 2 + yh_me, x_me * NYH + y_src // NYL))
-        return carry
-
-    lax.fori_loop(0, NY, greet_y, 0)
-
-    def greet_z(z_src, carry):
-        @pl.when(jnp.logical_or(z_src != z_me, core != z_core))
-        def _():
-            greet(((yl_me * NZ + z_src) * 2 + z_core, grp))
-        return carry
-
-    lax.fori_loop(0, NZ, greet_z, 0)
 
     loads[0].wait()
     greeted = (
@@ -279,10 +278,6 @@
     x_copy(slot_rows(-1, core), 4, 0, sibling)
     x_wait(slot_rows(1, core, 0), 2, 0)
     x_copy(slot_rows(1, core), 5, 0, sibling)
-    for half in (0, 1):
-        x_wait(slot_rows(2, core, half), 3, half)
-    x_copy(slot_rows(2, core), 6, 0, sibling)
-
     def pairs(slot, own=False):
         row = st[slot]
         same = same_label(slot, own)
@@ -314,6 +309,10 @@
             else:
                 target, device = x_to * 2 + which, x_peer(step, which)
             remote(gzs.at[target], gzg.at[own_rows, :], g_send, g_recv, device).start()
+        if step == 2:
+            for half in (0, 1):
+                x_wait(slot_rows(2, core, half), 3, half)
+            x_copy(slot_rows(2, core), 6, 0, sibling)
     gzg[own_rows, :] = gzs[own_x]
 
     x_wait(slot_rows(0, 1 - core), 0, 0)

time: 69.5 us -> 69.7 us (level)
  the two profiles are of different devices: /device:TPU:17 before, /device:TPU:8 now
where the time goes in v5:
time: 69.7 us; the launch traced here: 69.5 us
  Pallas kernels  68.9 us (99%)
    pallas_call x1, Pallas kernels, on_device(): pl.pallas_call(kernel, out_shape=(pltpu.VMEM((ROWS,), F32), pltpu.VMEM((Z...  68.3 us

profile of v5, /device:TPU:8, one launch (start us, length us, event | category | flops | bytes accessed | tf_op | source)
XLA Modules:
  0.0 69.5 jit_solution(17939563485280804609)
XLA Ops:
  0.6 68.3 %contrastive_loss_and_head_gradient.1 = (f32[192]{0:T(256)S(1)}, f32[10,128]{1,0:T(8,128)S(1)}) custom-call(bf16[192,1280]{1,0:T(8,128)(2,1)} %emb_hbm.1, bf16[1280,1024]{1,0:T(8,128)(2,1)} %w_hbm.1, s32[1536,128]{1,0:T(8,128)} %bitcast.2, s32[1536,128]{1,0:T(8,128)} %bitcast.3), custom_call_target="tpu_custom_call" | custom-call | tf_op jit(solution)/shard_map/contrastive_loss_and_head_gradient/pallas_call | solution.py:442
  68.9 0.6 hand_out.1

commit v6 on v4

--- a/solution.py
+++ b/solution.py
@@ -175,12 +175,6 @@
     def x_wait(rows, recv, half):
         remote(embg.at[rows, :], embg.at[rows, :], x_send, x_recv.at[recv, half], sibling).wait_recv()
 
-    x_copy(own_rows, 0, 0, sibling)
-    for half in (0, 1):
-        x_copy(slot_rows(0, core, half), 1, half, right)
-    for half in (1, 0):
-        x_copy(slot_rows(0, core, half), 2, half, left)
-
     for load in loads[5:]:
         load.wait()
     odd = lax.rem(grp, 2) == 1
@@ -231,6 +225,12 @@
         halo_wait(6, p)
         halo(6, 8, p, behind)
         halo(6, 5 + 2 * core, p, sibling)
+        if p == 1:
+            x_copy(own_rows, 0, 0, sibling)
+            for half in (0, 1):
+                x_copy(slot_rows(0, core, half), 1, half, right)
+            for half in (1, 0):
+                x_copy(slot_rows(0, core, half), 2, half, left)
     x_wait(slot_rows(-1, core, 0), 1, 0)
     x_copy(slot_rows(-1, core, 0), 3, 0, right)
     x_wait(slot_rows(1, core, 1), 2, 1)
@@ -279,10 +279,6 @@
     x_copy(slot_rows(-1, core), 4, 0, sibling)
     x_wait(slot_rows(1, core, 0), 2, 0)
     x_copy(slot_rows(1, core), 5, 0, sibling)
-    for half in (0, 1):
-        x_wait(slot_rows(2, core, half), 3, half)
-    x_copy(slot_rows(2, core), 6, 0, sibling)
-
     def pairs(slot, own=False):
         row = st[slot]
         same = same_label(slot, own)
@@ -314,6 +310,10 @@
             else:
                 target, device = x_to * 2 + which, x_peer(step, which)
             remote(gzs.at[target], gzg.at[own_rows, :], g_send, g_recv, device).start()
+        if step == 2:
+            for half in (0, 1):
+                x_wait(slot_rows(2, core, half), 3, half)
+            x_copy(slot_rows(2, core), 6, 0, sibling)
     gzg[own_rows, :] = gzs[own_x]
 
     x_wait(slot_rows(0, 1 - core), 0, 0)

time: 69.5 us -> 69.7 us (level)
  no operation moved by 1% of the time
where the time goes in v6:
time: 69.7 us; the launch traced here: 69.5 us
  Pallas kernels  68.9 us (99%)
    pallas_call x1, Pallas kernels, on_device(): pl.pallas_call(kernel, out_shape=(pltpu.VMEM((ROWS,), F32), pltpu.VMEM((Z...  68.3 us

profile of v6, /device:TPU:17, one launch (start us, length us, event | category | flops | bytes accessed | tf_op | source)
XLA Modules:
  0.0 69.5 jit_solution(16230588580494728352)
XLA Ops:
  0.6 68.3 %contrastive_loss_and_head_gradient.1 = (f32[192]{0:T(256)S(1)}, f32[10,128]{1,0:T(8,128)S(1)}) custom-call(bf16[192,1280]{1,0:T(8,128)(2,1)} %emb_hbm.1, bf16[1280,1024]{1,0:T(8,128)(2,1)} %w_hbm.1, s32[1536,128]{1,0:T(8,128)} %bitcast.2, s32[1536,128]{1,0:T(8,128)} %bitcast.3), custom_call_target="tpu_custom_call" | custom-call | tf_op jit(solution)/shard_map/contrastive_loss_and_head_gradient/pallas_call | solution.py:443
  68.9 0.6 hand_out.1
